TPU v7x, 32 devices: a whole 2x2x4 slice. The times are simulated.
32 devices in a mesh: frame: 4 (over y, core), video: 8 (over z, x).
Axes of the slice: x: 2, y: 2, z: 4, core: 2. Of those that a mesh axis runs over, the one named last changes fastest.
Arguments:
- frames: bfloat16 [16, 16, 197, 768], P('video', 'frame'), may hold values from -6 to 6
- out_cotangent: bfloat16 [16, 16, 197, 768], P('video', 'frame'), may hold values from -6 to 6
- frame_counts: int32 [16], P('video'), may hold values from 8 to 16, as said below
- message_proj: bfloat16 [768, 768], replicated, may hold values from -0.21875 to 0.21875
- message_gain: float32 [768], replicated, may hold values from 0.5 to 1.5
- message_qkv: bfloat16 [768, 2304], replicated, may hold values from -0.21875 to 0.21875
- message_out: bfloat16 [768, 768], replicated, may hold values from -0.625 to 0.625
- attn_gain: float32 [768], replicated, may hold values from 0.5 to 1.5
- attn_qkv: bfloat16 [768, 2304], replicated, may hold values from -0.21875 to 0.21875
- attn_out: bfloat16 [768, 768], replicated, may hold values from -0.875 to 0.875
- mlp_gain: float32 [768], replicated, may hold values from 0.5 to 1.5
- mlp_up: bfloat16 [768, 3072], replicated, may hold values from -0.21875 to 0.21875
- mlp_down: bfloat16 [3072, 768], replicated, may hold values from -0.21875 to 0.21875
Outputs:
- encoded: bfloat16 [16, 16, 197, 768], P('video', 'frame')
- frames_grad: float32 [16, 16, 197, 768], P('video', 'frame')
- message_proj_grad: float32 [768, 768], P('video')
- message_gain_grad: float32 [768], P('video')
- message_qkv_grad: float32 [768, 2304], P('video')
- message_out_grad: float32 [768, 768], P('video')
- attn_gain_grad: float32 [768], P('video')
- attn_qkv_grad: float32 [768, 2304], P('video')
- attn_out_grad: float32 [768, 768], P('video')
- mlp_gain_grad: float32 [768], P('video')
- mlp_up_grad: float32 [768, 3072], P('video')
- mlp_down_grad: float32 [3072, 768], P('video')
Inputs may be any that keep to these rules, and one draw needn't show every extreme that they name: `frame_counts`: each video has 8 or 16 frames, held in its first frame slots; among the 2 videos at each index of video at least one has 16.
All inputs are finite; a program needn't handle non-finite values.
Results may differ from a plain program's by a relative error of at most 0.028.
Values may be sent and summed in bfloat16 or wider, within the bound.
No kernel may reach another device: no remote copies, remote signals or barrier semaphores. Data moves between devices by JAX's collectives and lax.ppermute only.
A program may use at most 256 MiB of HBM per device.

v0:
```python
import math

import jax
import jax.numpy as jnp
from jax import lax
from jax.sharding import PartitionSpec as P

H = 12
HD = 64


EPSILON = 1e-05


def dot_plain(left, right):
    return jnp.dot(left, right, preferred_element_type=jnp.float32)


def dot_rows(left, right):
    return lax.dot_general(
        left, right, (((0,), (0,)), ((), ())), preferred_element_type=jnp.float32
    )


def dot_back(left, right):
    return lax.dot_general(
        left, right, (((1,), (1,)), ((), ())), preferred_element_type=jnp.float32
    )


def norm_forward(value, gain):
    centre = jnp.mean(value, axis=-1, keepdims=True)
    centred = value - centre
    spread = jnp.mean(centred * centred, axis=-1, keepdims=True)
    inverse = lax.rsqrt(spread + EPSILON)
    normal = centred * inverse
    return (normal * gain, normal, inverse)


def norm_backward(upstream, normal, inverse, gain):
    scaled = upstream * gain
    inner = (
        scaled
        - jnp.mean(scaled, axis=-1, keepdims=True)
        - normal * jnp.mean(scaled * normal, axis=-1, keepdims=True)
    )
    return (inner * inverse, jnp.sum(upstream * normal, axis=0))


def frame_attend(block):
    queries, keys, values = block
    scale = 1.0 / math.sqrt(HD)
    scores = (
        jnp.einsum("fqhd,fkhd->fhqk", queries, keys, preferred_element_type=jnp.float32) * scale
    )
    score_top = jnp.max(scores, axis=-1, keepdims=True)
    raised = jnp.exp(scores - score_top)
    raised_total = jnp.sum(raised, axis=-1, keepdims=True)
    log_total = score_top + jnp.log(raised_total)
    weight_low = (raised / raised_total).astype(jnp.bfloat16)
    context = jnp.einsum("fhqk,fkhd->fqhd", weight_low, values, preferred_element_type=jnp.float32)
    return (context.astype(jnp.bfloat16), log_total)


def frame_attend_back(block):
    queries, keys, values, context_grad, log_total = block
    scale = 1.0 / math.sqrt(HD)
    scores_again = (
        jnp.einsum("fqhd,fkhd->fhqk", queries, keys, preferred_element_type=jnp.float32) * scale
    )
    weight_again = jnp.exp(scores_again - log_total)
    weight_again_low = weight_again.astype(jnp.bfloat16)
    value_grad = jnp.einsum(
        "fhqk,fqhd->fkhd", weight_again_low, context_grad, preferred_element_type=jnp.float32
    )
    weight_grad = jnp.einsum(
        "fqhd,fkhd->fhqk", context_grad, values, preferred_element_type=jnp.float32
    )
    score_grad = weight_again * (
        weight_grad - jnp.sum(weight_again * weight_grad, axis=-1, keepdims=True)
    )
    score_low = score_grad.astype(jnp.bfloat16)
    query_grad = (
        jnp.einsum("fhqk,fkhd->fqhd", score_low, keys, preferred_element_type=jnp.float32) * scale
    )
    key_grad = (
        jnp.einsum("fhqk,fqhd->fkhd", score_low, queries, preferred_element_type=jnp.float32)
        * scale
    )
    return jnp.stack([query_grad, key_grad, value_grad], axis=2).astype(jnp.bfloat16)


def on_device(
    frames,
    out_cotangent,
    frame_counts,
    message_proj,
    message_gain,
    message_qkv,
    message_out,
    attn_gain,
    attn_qkv,
    attn_out,
    mlp_gain,
    mlp_up,
    mlp_down,
):
    videos, slots, patches, width = frames.shape
    tokens = patches + 1
    scale = 1.0 / math.sqrt(HD)
    group_size = lax.axis_size("frame")
    slot_ids = lax.axis_index("frame") * slots + jnp.arange(slots, dtype=jnp.int32)
    alive = (slot_ids[None, :] < frame_counts[:, None]).astype(jnp.float32)
    key_keep = jnp.arange(slots * group_size, dtype=jnp.int32)[None, :] < frame_counts[:, None]
    frame_total = videos * slots
    row_total = frame_total * tokens
    block_frames = math.gcd(frame_total, 4)
    block_count = frame_total // block_frames
    class_rows = frames[:, :, 0, :].reshape(frame_total, width)
    message_pre = dot_plain(class_rows, message_proj)
    message, message_normal, message_inverse = norm_forward(message_pre, message_gain)
    message_low = message.astype(jnp.bfloat16)
    gathered = lax.all_gather(
        message_low.reshape(videos, slots, width), "frame", axis=1, tiled=True
    )
    all_frames = gathered.shape[1]
    own_query = (
        dot_plain(message_low, message_qkv[:, :width])
        .astype(jnp.bfloat16)
        .reshape(videos, slots, H, HD)
    )
    key_value = dot_plain(
        gathered.reshape(videos * all_frames, width), message_qkv[:, width:]
    ).astype(jnp.bfloat16)
    key_value = key_value.reshape(videos, all_frames, 2, H, HD)
    message_key = key_value[:, :, 0]
    message_value = key_value[:, :, 1]
    message_score = (
        jnp.einsum("vqhd,vkhd->vhqk", own_query, message_key, preferred_element_type=jnp.float32)
        * scale
    )
    message_score = jnp.where(key_keep[:, None, None, :], message_score, -1e30)
    message_weight = jax.nn.softmax(message_score, axis=-1)
    message_weight_low = message_weight.astype(jnp.bfloat16)
    mcontext = jnp.einsum(
        "vhqk,vkhd->vqhd", message_weight_low, message_value, preferred_element_type=jnp.float32
    )
    mcontext = mcontext.astype(jnp.bfloat16).reshape(frame_total, width)
    message_two = message + dot_plain(mcontext, message_out)
    stream = jnp.concatenate(
        [frames.reshape(frame_total, patches, width).astype(jnp.float32), message_two[:, None, :]],
        axis=1,
    )
    stream_flat = stream.reshape(row_total, width)
    normed_one, normal_one, inverse_one = norm_forward(stream_flat, attn_gain)
    normed_one_low = normed_one.astype(jnp.bfloat16)
    triple = (
        dot_plain(normed_one_low, attn_qkv)
        .astype(jnp.bfloat16)
        .reshape(block_count, block_frames, tokens, 3, H, HD)
    )
    queries = triple[:, :, :, 0]
    keys = triple[:, :, :, 1]
    values = triple[:, :, :, 2]
    context, log_total = lax.map(frame_attend, (queries, keys, values))
    context = context.reshape(row_total, width)
    hidden = stream_flat + dot_plain(context, attn_out)
    normed_two, normal_two, inverse_two = norm_forward(hidden, mlp_gain)
    normed_two_low = normed_two.astype(jnp.bfloat16)
    up_value = dot_plain(normed_two_low, mlp_up)
    sigma = jax.nn.sigmoid(1.702 * up_value)
    activation_low = (up_value * sigma).astype(jnp.bfloat16)
    final = hidden + dot_plain(activation_low, mlp_down)
    final = final.reshape(videos, slots, tokens, width)[:, :, :patches, :] * alive[:, :, None, None]
    encoded = final.astype(jnp.bfloat16)
    final_grad = out_cotangent.astype(jnp.float32) * alive[:, :, None, None]
    final_grad = jnp.concatenate(
        [final_grad, jnp.zeros((videos, slots, 1, width), jnp.float32)], axis=2
    ).reshape(row_total, width)
    final_low = final_grad.astype(jnp.bfloat16)
    down_weight_grad = dot_rows(activation_low, final_low)
    activation_grad = dot_back(final_low, mlp_down)
    up_grad = (activation_grad * (sigma + 1.702 * up_value * sigma * (1.0 - sigma))).astype(
        jnp.bfloat16
    )
    up_weight_grad = dot_rows(normed_two_low, up_grad)
    normed_two_grad = dot_back(up_grad, mlp_up)
    hidden_part, mlp_gain_grad = norm_backward(normed_two_grad, normal_two, inverse_two, mlp_gain)
    hidden_grad = final_grad + hidden_part
    hidden_low = hidden_grad.astype(jnp.bfloat16)
    out_weight_grad = dot_rows(context, hidden_low)
    context_grad = (
        dot_back(hidden_low, attn_out)
        .astype(jnp.bfloat16)
        .reshape(block_count, block_frames, tokens, H, HD)
    )
    triple_grad = lax.map(frame_attend_back, (queries, keys, values, context_grad, log_total))
    triple_grad = triple_grad.reshape(row_total, 3 * width)
    qkv_weight_grad = dot_rows(normed_one_low, triple_grad)
    normed_one_grad = dot_back(triple_grad, attn_qkv)
    stream_part, attn_gain_grad = norm_backward(normed_one_grad, normal_one, inverse_one, attn_gain)
    stream_grad = (hidden_grad + stream_part).reshape(frame_total, tokens, width)
    message_two_grad = stream_grad[:, patches, :]
    message_two_low = message_two_grad.astype(jnp.bfloat16)
    message_out_weight_grad = dot_rows(mcontext, message_two_low)
    mcontext_grad = (
        dot_back(message_two_low, message_out).astype(jnp.bfloat16).reshape(videos, slots, H, HD)
    )
    mvalue_part = jnp.einsum(
        "vhqk,vqhd->vkhd", message_weight_low, mcontext_grad, preferred_element_type=jnp.float32
    )
    mweight_grad = jnp.einsum(
        "vqhd,vkhd->vhqk", mcontext_grad, message_value, preferred_element_type=jnp.float32
    )
    mscore_grad = message_weight * (
        mweight_grad - jnp.sum(message_weight * mweight_grad, axis=-1, keepdims=True)
    )
    mscore_low = mscore_grad.astype(jnp.bfloat16)
    mquery_grad = (
        jnp.einsum("vhqk,vkhd->vqhd", mscore_low, message_key, preferred_element_type=jnp.float32)
        * scale
    )
    mkey_part = (
        jnp.einsum("vhqk,vqhd->vkhd", mscore_low, own_query, preferred_element_type=jnp.float32)
        * scale
    )
    mkey_sum, mvalue_sum = (
        lax.psum_scatter(
            mkey_part.reshape(videos, all_frames, width).astype(jnp.bfloat16),
            "frame",
            scatter_dimension=1,
            tiled=True,
        ).astype(jnp.float32),
        lax.psum_scatter(
            mvalue_part.reshape(videos, all_frames, width).astype(jnp.bfloat16),
            "frame",
            scatter_dimension=1,
            tiled=True,
        ).astype(jnp.float32),
    )
    mtriple_grad = jnp.concatenate(
        [
            mquery_grad.reshape(frame_total, width),
            mkey_sum.reshape(frame_total, width),
            mvalue_sum.reshape(frame_total, width),
        ],
        axis=1,
    ).astype(jnp.bfloat16)
    mqkv_weight_grad = dot_rows(message_low, mtriple_grad)
    message_grad = message_two_grad + dot_back(mtriple_grad, message_qkv)
    pre_part, message_gain_grad = norm_backward(
        message_grad, message_normal, message_inverse, message_gain
    )
    pre_low = pre_part.astype(jnp.bfloat16)
    proj_weight_grad = dot_rows(class_rows, pre_low)
    class_grad = dot_back(pre_low, message_proj)
    patch_grad = stream_grad[:, :patches, :]
    patch_grad = jnp.concatenate(
        [(patch_grad[:, 0, :] + class_grad)[:, None, :], patch_grad[:, 1:, :]], axis=1
    )
    frames_grad = patch_grad.reshape(videos, slots, patches, width)
    every_sum = (
        lax.psum_scatter(
            proj_weight_grad.astype(jnp.bfloat16), "video", scatter_dimension=0, tiled=True
        ).astype(jnp.float32),
        lax.psum_scatter(
            message_gain_grad.astype(jnp.bfloat16), "video", scatter_dimension=0, tiled=True
        ).astype(jnp.float32),
        lax.psum_scatter(
            mqkv_weight_grad.astype(jnp.bfloat16), "video", scatter_dimension=0, tiled=True
        ).astype(jnp.float32),
        lax.psum_scatter(
            message_out_weight_grad.astype(jnp.bfloat16), "video", scatter_dimension=0, tiled=True
        ).astype(jnp.float32),
        lax.psum_scatter(
            attn_gain_grad.astype(jnp.bfloat16), "video", scatter_dimension=0, tiled=True
        ).astype(jnp.float32),
        lax.psum_scatter(
            qkv_weight_grad.astype(jnp.bfloat16), "video", scatter_dimension=0, tiled=True
        ).astype(jnp.float32),
        lax.psum_scatter(
            out_weight_grad.astype(jnp.bfloat16), "video", scatter_dimension=0, tiled=True
        ).astype(jnp.float32),
        lax.psum_scatter(
            mlp_gain_grad.astype(jnp.bfloat16), "video", scatter_dimension=0, tiled=True
        ).astype(jnp.float32),
        lax.psum_scatter(
            up_weight_grad.astype(jnp.bfloat16), "video", scatter_dimension=0, tiled=True
        ).astype(jnp.float32),
        lax.psum_scatter(
            down_weight_grad.astype(jnp.bfloat16), "video", scatter_dimension=0, tiled=True
        ).astype(jnp.float32),
    )
    every_sum = (
        lax.psum(every_sum[0].astype(jnp.bfloat16), "frame").astype(jnp.float32),
        lax.psum(every_sum[1].astype(jnp.bfloat16), "frame").astype(jnp.float32),
        lax.psum(every_sum[2].astype(jnp.bfloat16), "frame").astype(jnp.float32),
        lax.psum(every_sum[3].astype(jnp.bfloat16), "frame").astype(jnp.float32),
        lax.psum(every_sum[4].astype(jnp.bfloat16), "frame").astype(jnp.float32),
        lax.psum(every_sum[5].astype(jnp.bfloat16), "frame").astype(jnp.float32),
        lax.psum(every_sum[6].astype(jnp.bfloat16), "frame").astype(jnp.float32),
        lax.psum(every_sum[7].astype(jnp.bfloat16), "frame").astype(jnp.float32),
        lax.psum(every_sum[8].astype(jnp.bfloat16), "frame").astype(jnp.float32),
        lax.psum(every_sum[9].astype(jnp.bfloat16), "frame").astype(jnp.float32),
    )
    (
        proj_sum,
        message_gain_sum,
        mqkv_sum,
        message_out_sum,
        attn_gain_sum,
        qkv_sum,
        out_sum,
        mlp_gain_sum,
        up_sum,
        down_sum,
    ) = every_sum
    return (
        encoded,
        frames_grad,
        proj_sum,
        message_gain_sum,
        mqkv_sum,
        message_out_sum,
        attn_gain_sum,
        qkv_sum,
        out_sum,
        mlp_gain_sum,
        up_sum,
        down_sum,
    )


def solution(mesh):
    return jax.shard_map(
        on_device,
        mesh=mesh,
        in_specs=(
            P("video", "frame", None, None),
            P("video", "frame", None, None),
            P("video"),
            P(),
            P(),
            P(),
            P(),
            P(),
            P(),
            P(),
            P(),
            P(),
            P(),
        ),
        out_specs=(
            P("video", "frame", None, None),
            P("video", "frame", None, None),
            P("video", None),
            P("video"),
            P("video", None),
            P("video", None),
            P("video"),
            P("video", None),
            P("video", None),
            P("video"),
            P("video", None),
            P("video", None),
        ),
        check_vma=False,
    )
```

profile of v0, /device:TPU:0, one launch (start us, length us, event | category | flops | bytes accessed | tf_op | source)
XLA Modules:
  0.0 1091.9 jit_solution(2944114531100151049)
XLA Ops:
  7.3 4.4 copy.118
  16.5 6.2 all_gather.3
  42.8 4.9 fusion.97
  47.7 4.2 reshape.370
  51.9 3.7 multiply_reduce_fusion.2
  57.1 11.4 %convolution_convert_fusion = bf16[1584,2304]{1,0:T(8,128)(2,1)} fusion(bf16[768,2304]{1,0:T(8,128)(2,1)S(1)} %copy-done, f32[1584,768]{1,0:T(8,128)} %reshape.370, f32[768]{0:T(1024)} %param.24, f32[1584]{0:T(1024)} %rsqrt.30, f32[1584]{0:T(1024)S(1)} %div.62), kind=kOutput, calls=%fused_computation.61 | convolution fusion | flops 5614202880 | bytes 15719808 | tf_op jit(solution)/shard_map/dot_general | solution.py:16
  68.4 11.8 %copy.126 = bf16[1584,2304]{0,1:T(8,128)(2,1)} copy(bf16[1584,2304]{1,0:T(8,128)(2,1)} %convolution_convert_fusion) | data formatting | bytes 14598144 | tf_op jit(solution)/shard_map/convert_element_type | solution.py:159
  80.2 19.3 %reshape.371 = bf16[2,4,198,3,12,64]{2,1,0,5,4,3:T(4,128)(2,1)} reshape(bf16[1584,2304]{0,1:T(8,128)(2,1)} %copy.126) | data formatting | bytes 14598144 | tf_op jit(solution)/shard_map/reshape | solution.py:160
  99.5 6.4 slice_bitcast_fusion
  113.2 21.1 %while.22 = (s32[]{:T(128)}, bf16[2,4,198,12,64]{2,1,0,4,3:T(4,128)(2,1)}, f32[2,4,12,198,1]{3,2,1,4,0:T(8,128)}, bf16[2,4,198,12,64]{2,4,3,1,0:T(8,128)(2,1)}, ...) while((s32[]{:T(128)}, bf16[2,4,198,12,64]{2,1,0,4,3:T(4,128)(2,1)}, ...), condition=%wide.region_9.10_spmd, body=%wide.region_6.9_spmd.sunk | while | flops 499273632 | bytes 44393000 | solution.py:165
  113.4 3.4 multiply_reduce_fusion.17
  123.9 3.4 multiply_reduce_fusion.17
  134.3 7.7 reshape.372
  142.0 5.7 fusion.102
  148.5 18.9 %multiply_convert_fusion.4 = (bf16[1584,3072]{1,0:T(8,128)(2,1)}, f32[1584,3072]{1,0:T(8,128)}) fusion(bf16[768,3072]{1,0:T(8,128)(2,1)} %param.28, f32[1584,768]{1,0:T(8,128)S(1)} %get-tuple-element.249, f32[768]{0:T(1024)S(1)} %copy-done.45, f32[1584]{0:T(1024)S(1)} %add_rsqrt_fusion, f32[1584]{0:T(1024)S(1)} %broadcast_multiply_fusion.4), kind=kOutput, calls=%fused_computation.59 | convolution fusion | flops 7508312064 | bytes 38796672 | tf_op jit(solution)/shard_map/dot_general | solution.py:16
  167.4 11.8 %convolution_add_fusion.1 = f32[1584,768]{1,0:T(8,128)} fusion(f32[1584,768]{1,0:T(8,128)S(1)} %get-tuple-element.249, bf16[1584,3072]{1,0:T(8,128)(2,1)} %get-tuple-element.250, bf16[3072,768]{1,0:T(8,128)(2,1)S(1)} %bitcast.202), kind=kOutput, calls=%fused_computation.87 | convolution fusion | flops 7475466240 | bytes 24182784 | tf_op jit(solution)/shard_map/dot_general | solution.py:16
  179.2 4.2 reshape.373
  184.1 5.3 convert_multiply_fusion
  192.1 4.2 reshape.374
  196.2 20.8 %multiply_convert_fusion.3 = bf16[1584,3072]{1,0:T(8,128)(2,1)} fusion(f32[1584,3072]{1,0:T(8,128)} %get-tuple-element.251, bf16[3072,768]{1,0:T(8,128)(2,1)} %param.29, f32[1584,768]{1,0:T(8,128)} %reshape.374), kind=kOutput, calls=%fused_computation.58 | convolution fusion | flops 7524126720 | bytes 38780928 | tf_op jit(solution)/shard_map/dot_general | solution.py:26
  217.0 16.1 %multiply_reduce_fusion.3 = (bf16[768]{0:T(1024)(128)(2,1)}, f32[1584]{0:T(1024)S(1)}, f32[1584]{0:T(1024)S(1)}, f32[1584,768]{1,0:T(8,128)S(1)}) fusion(f32[1584,768]{1,0:T(8,128)} %copy-done.9, f32[1584]{0:T(1024)S(1)} %add_rsqrt_fusion, f32[1584]{0:T(1024)S(1)} %broadcast_multiply_fusion.4, f32[768]{0:T(1024)} %param.27, ...), kind=kOutput, calls=%fused_computation.72 | convolution fusion | flops 7483977728 | bytes 24212736 | tf_op jit(solution)/shard_map/dot_general | solution.py:26
  233.2 4.3 multiply_add_fusion.1
  239.6 3.6 convolution_convert_fusion.5
  243.2 8.4 reshape.383
  251.6 8.6 copy.135
  260.2 82.2 %while.23 = (s32[]{:T(128)}, bf16[2,4,198,3,12,64]{2,1,0,5,4,3:T(4,128)(2,1)}, bf16[2,4,198,12,64]{2,4,3,1,0:T(8,128)(2,1)}, bf16[2,4,198,12,64]{2,4,3,1,0:T(8,1...) while((s32[]{:T(128)}, ...), condition=%wide.region_16.17_spmd, body=%wide.region_14.16_spmd.sunk | while | flops 1233609728 | bytes 184037200 | solution.py:197
  260.7 3.5 fusion.169
  264.5 6.5 multiply_reduce_fusion.18
  271.0 11.4 %multiply_convert_fusion.15 = bf16[4,12,198,198]{2,3,1,0:T(8,128)(2,1)} fusion(f32[4,12,198,198]{2,3,1,0:T(8,128)} %get-tuple-element.345, f32[4,12,198,198]{2,3,1,0:T(8,128)} %copy-done.1, f32[4,12,198]{2,1,0:T(8,128)} %get-tuple-element.346, f32[4,12,198]{2,1,0:T(8,128)} %copy-done.7), kind=kLoop, calls=%fused_computation.19.clone.1 | loop fusion | flops 9408960 | bytes 18893952 | tf_op jit(solution)/shard_map/while/body/eval_jaxpr/convert_element_type | solution.py:82
  282.5 4.1 fusion.172
  286.6 5.1 fusion.171
  294.7 6.7 copy_dynamic-update-slice_fusion.5
  301.5 3.5 fusion.169
  305.3 6.5 multiply_reduce_fusion.18
  311.9 11.4 %multiply_convert_fusion.15 = bf16[4,12,198,198]{2,3,1,0:T(8,128)(2,1)} fusion(f32[4,12,198,198]{2,3,1,0:T(8,128)} %get-tuple-element.345, f32[4,12,198,198]{2,3,1,0:T(8,128)} %copy-done.1, f32[4,12,198]{2,1,0:T(8,128)} %get-tuple-element.346, f32[4,12,198]{2,1,0:T(8,128)} %copy-done.7), kind=kLoop, calls=%fused_computation.19.clone.1 | loop fusion | flops 9408960 | bytes 18893952 | tf_op jit(solution)/shard_map/while/body/eval_jaxpr/convert_element_type | solution.py:82
  323.3 4.1 fusion.172
  327.4 5.1 fusion.171
  335.6 6.8 copy_dynamic-update-slice_fusion.5
  342.5 16.6 %reshape.376 = bf16[1584,2304]{0,1:T(8,128)(2,1)} reshape(bf16[2,4,198,3,12,64]{2,1,0,5,4,3:T(4,128)(2,1)} %get-tuple-element.84) | data formatting | bytes 14598144 | tf_op jit(solution)/shard_map/reshape | solution.py:198
  359.1 14.0 %multiply_reduce_fusion.4 = (bf16[768]{0:T(1024)(128)(2,1)}, f32[1584]{0:T(1024)S(1)}, f32[1584]{0:T(1024)S(1)}, f32[1584,768]{1,0:T(8,128)S(1)}) fusion(f32[1584,768]{1,0:T(8,128)} %reshape.370, f32[1584]{0:T(1024)S(1)} %copy-done.39, f32[1584]{0:T(1024)S(1)} %copy-done.38, f32[768]{0:T(1024)} %param.24, bf16[1584,2304]{0,1:T(8,128)(2,1)} %reshape.376, ...), kind=kOutput, calls=%fused_computation.73 | convolution fusion | flops 5615415296 | bytes 20600064 | tf_op jit(solution)/shard_map/dot_general | solution.py:26
  373.2 3.3 multiply_add_fusion
  376.4 4.2 reshape.377
  404.5 26.7 %all-reduce.13.cloned.1.call-done = (bf16[2,16,768]{2,1,0:T(8,128)(2,1)}, bf16[2,16,768]{2,1,0:T(8,128)(2,1)}) async-done(((bf16[2,16,768]{2,1,0:T(8,128)(2,1)}, bf16[2,16,768]{2,1,0:T(8,128)(2,1)}), (bf16[2,16,768]{2,1,0:T(8,128)(2,1)}, bf16[2,16,768]{2,1,0:T(8,128)(2,1)})) %all-reduce.13.cloned.1.call-update) | async-done | bytes 98320
  439.2 3.7 multiply_reduce_fusion.11
  448.3 6.5 convolution_convert_fusion.8
  457.2 3.9 multiply_convert_fusion.5
  461.1 3.1 convert_element_type.259
  464.2 11.7 %convolution_convert_fusion.3 = bf16[768,2304]{1,0:T(8,128)(2,1)} fusion(bf16[1584,768]{1,0:T(8,128)(2,1)} %convert_element_type.259, bf16[1584,2304]{0,1:T(8,128)(2,1)} %reshape.376), kind=kOutput, calls=%fused_computation.64 | convolution fusion | flops 5607456768 | bytes 13271040 | tf_op jit(solution)/shard_map/dot_general | solution.py:20
  476.0 3.6 convolution_convert_fusion.4
  480.0 14.8 %convolution_convert_fusion.2 = bf16[768,3072]{1,0:T(8,128)(2,1)} fusion(bf16[1584,3072]{1,0:T(8,128)(2,1)} %multiply_convert_fusion.3, f32[1584,768]{1,0:T(8,128)} %copy-done.9, f32[768]{0:T(1024)S(1)} %copy-done.47, f32[1584]{0:T(1024)} %copy-done.36, f32[1584]{0:T(1024)} %copy-done.30), kind=kOutput, calls=%fused_computation.63 | convolution fusion | flops 7481475072 | bytes 19332480 | tf_op jit(solution)/shard_map/dot_general | solution.py:20
  494.9 14.4 %convolution_convert_fusion.1 = bf16[3072,768]{1,0:T(8,128)(2,1)} fusion(bf16[1584,3072]{1,0:T(8,128)(2,1)} %get-tuple-element.250, f32[1584,768]{1,0:T(8,128)} %reshape.374), kind=kOutput, calls=%fused_computation.62 | convolution fusion | flops 7477825536 | bytes 19316736 | tf_op jit(solution)/shard_map/dot_general | solution.py:20
  509.7 2.8 reduce-scatter.24.cloned.1.call-done
  514.3 65.8 %reduce-scatter.18.cloned.1.call-done = bf16[96,768]{1,0:T(8,128)(2,1)} async-done(((bf16[768,768]{1,0:T(8,128)(2,1)}), bf16[96,768]{1,0:T(8,128)(2,1)}) %reduce-scatter.18.cloned.1.call-update) | async-done | bytes 147472 | tf_op jit(solution)/shard_map/reduce_scatter | solution.py:281
  580.1 67.2 %reduce-scatter.14.cloned.1.call-done = bf16[96,768]{1,0:T(8,128)(2,1)} async-done(((bf16[768,768]{1,0:T(8,128)(2,1)}), bf16[96,768]{1,0:T(8,128)(2,1)}) %reduce-scatter.14.cloned.1.call-update) | async-done | bytes 147472 | tf_op jit(solution)/shard_map/reduce_scatter | solution.py:272
  647.3 82.1 %reduce-scatter.16.cloned.1.call-done = bf16[96,2304]{1,0:T(8,128)(2,1)} async-done(((bf16[768,2304]{1,0:T(8,128)(2,1)}), bf16[96,2304]{1,0:T(8,128)(2,1)}) %reduce-scatter.16.cloned.1.call-update) | async-done | bytes 442384 | tf_op jit(solution)/shard_map/reduce_scatter | solution.py:278
  729.4 82.6 %reduce-scatter.12.cloned.1.call-done = bf16[96,2304]{1,0:T(8,128)(2,1)} async-done(((bf16[768,2304]{1,0:T(8,128)(2,1)}), bf16[96,2304]{1,0:T(8,128)(2,1)}) %reduce-scatter.12.cloned.1.call-update) | async-done | bytes 442384 | tf_op jit(solution)/shard_map/reduce_scatter | solution.py:269
  812.1 99.5 %reduce-scatter.20.cloned.1.call-done = bf16[96,3072]{1,0:T(8,128)(2,1)} async-done(((bf16[768,3072]{1,0:T(8,128)(2,1)}), bf16[96,3072]{1,0:T(8,128)(2,1)}) %reduce-scatter.20.cloned.1.call-update) | async-done | bytes 589840 | tf_op jit(solution)/shard_map/reduce_scatter | solution.py:287
  911.5 99.3 %reduce-scatter.22.cloned.1.call-done = bf16[384,768]{1,0:T(8,128)(2,1)} async-done(((bf16[3072,768]{1,0:T(8,128)(2,1)}), bf16[384,768]{1,0:T(8,128)(2,1)}) %reduce-scatter.22.cloned.1.call-update) | async-done | bytes 589840 | tf_op jit(solution)/shard_map/reduce_scatter | solution.py:290
  1010.9 2.8 slice.59
  1014.3 4.0 copy.147
  1021.4 21.0 %all-reduce.6 = (bf16[768]{0:T(1024)(128)(2,1)}, bf16[768]{0:T(1024)(128)(2,1)}, bf16[768]{0:T(1024)(128)(2,1)}) all-reduce(bf16[768]{0:T(1024)(128)(2,1)S(1)} %copy-done.44, bf16[768]{0:T(1024)(128)(2,1)} %get-tuple-element.181, bf16[768]{0:T(1024)(128)(2,1)} %get-tuple-element.179), channel_id=5, replica_groups=mesh['frame'=4,'video'=8] {'video'}, use_global_device_ids=true, to_apply=%region_27.28.clone | all-reduce | flops 2304 | bytes 9216
  1045.7 6.3 all-reduce.7
  1059.2 5.7 pad_maximum_fusion.2
  1064.8 9.5 all-reduce.15.cloned.1.call-done
  (248 shorter events, 125.9 us)
Async XLA Ops:
  7.2 49.9 %copy-start = (bf16[768,2304]{1,0:T(8,128)(2,1)S(1)}, bf16[768,2304]{1,0:T(8,128)(2,1)}, u32[]{:S(2)}) copy-start(bf16[768,2304]{1,0:T(8,128)(2,1)} %param.25) | copy-start | bytes 10616836
  7.2 4.5 slice-start
  7.2 7.9 copy-start.33
  7.2 424.0 %all-reduce.13.cloned.1.call-start = ((), (), s32[]{:S(2)}) async-start(), calls=%async_computation.14 | async-start | bytes 196608
  15.2 32.5 %copy-start.21 = (bf16[8,768]{1,0:T(8,128)(2,1)}, bf16[8,768]{1,0:T(8,128)(2,1)S(1)}, u32[]{:S(2)}) copy-start(bf16[8,768]{1,0:T(8,128)(2,1)S(1)} %multiply_convert_fusion.11) | copy-start | bytes 36868
  47.7 7.9 copy-start.25
  55.6 12.8 %copy-start.37 = (f32[1584]{0:T(1024)}, f32[1584]{0:T(1024)S(1)}, u32[]{:S(2)}) copy-start(f32[1584]{0:T(1024)S(1)} %div.62) | copy-start | bytes 19012
  56.4 12.0 %copy-start.31 = (f32[8,198]{1,0:T(8,128)}, f32[8,198]{1,0:T(8,128)S(1)}, u32[]{:S(2)}) copy-start(f32[8,198]{1,0:T(8,128)S(1)} %add_rsqrt_fusion.1) | copy-start | bytes 19012
  116.9 2.1 copy-start.16
  116.9 2.1 copy-start.5
  119.0 2.5 copy-start.17
  127.3 2.1 copy-start.5
  129.4 2.5 copy-start.17
  147.7 19.7 %copy-start.9 = (f32[1584,768]{1,0:T(8,128)}, f32[1584,768]{1,0:T(8,128)S(1)}, u32[]{:S(2)}) copy-start(f32[1584,768]{1,0:T(8,128)S(1)} %get-tuple-element.249) | copy-start | bytes 14598148
  147.8 85.4 %copy-start.30 = (f32[1584]{0:T(1024)}, f32[1584]{0:T(1024)S(1)}, u32[]{:S(2)}) copy-start(f32[1584]{0:T(1024)S(1)} %broadcast_multiply_fusion.4) | copy-start | bytes 19012
  147.8 19.6 %slice-start.1 = ((s8[4718592]{0:T(1024)(128)(4,1)}), s8[4194304]{0:T(1024)(128)(4,1)S(1)}, s32[]{:S(2)}) async-start(s8[4718592]{0:T(1024)(128)(4,1)} %bitcast.201), calls=%async_computation.17 | async-start | bytes 8388608
  148.5 84.7 %copy-start.36 = (f32[1584]{0:T(1024)}, f32[1584]{0:T(1024)S(1)}, u32[]{:S(2)}) copy-start(f32[1584]{0:T(1024)S(1)} %add_rsqrt_fusion) | copy-start | bytes 19012
  148.5 18.9 %slice-start.2 = ((s8[4718592]{0:T(1024)(128)(4,1)}), s8[524288]{0:T(1024)(128)(4,1)S(1)}, s32[]{:S(2)}) async-start(s8[4718592]{0:T(1024)(128)(4,1)} %bitcast.201), calls=%async_computation.18 | async-start | bytes 1048576
  217.0 16.1 %copy-start.10 = (f32[1584,768]{1,0:T(8,128)S(1)}, f32[1584,768]{1,0:T(8,128)}, u32[]{:S(2)}) copy-start(f32[1584,768]{1,0:T(8,128)} %reshape.374) | copy-start | bytes 14598148
  217.0 16.1 %copy-start.46 = (f32[768]{0:T(1024)S(1)}, f32[768]{0:T(1024)}, u32[]{:S(2)}) copy-start(f32[768]{0:T(1024)} %param.27) | copy-start | bytes 9220
  233.2 6.5 copy-start.48
  237.4 2.2 copy-start.12
  260.6 3.6 copy-start.18
  260.6 3.6 copy-start.3
  260.7 3.8 copy-start.6
  264.2 6.8 copy-start.1
  264.2 6.8 copy-start.7
  282.5 9.3 copy-start.2
  286.6 5.2 copy-start.4
  286.6 5.2 copy-start.8
  301.5 3.5 copy-start.18
  301.5 3.6 copy-start.3
  301.5 3.9 copy-start.6
  305.0 6.8 copy-start.1
  305.0 6.8 copy-start.7
  323.3 9.3 copy-start.2
  327.4 5.2 copy-start.4
  327.4 5.2 copy-start.8
  342.5 16.6 %copy-start.38 = (f32[1584]{0:T(1024)S(1)}, f32[1584]{0:T(1024)}, u32[]{:S(2)}) copy-start(f32[1584]{0:T(1024)} %copy-done.37) | copy-start | bytes 19012
  342.5 16.6 %copy-start.39 = (f32[1584]{0:T(1024)S(1)}, f32[1584]{0:T(1024)}, u32[]{:S(2)}) copy-start(f32[1584]{0:T(1024)} %rsqrt.30) | copy-start | bytes 19012
  359.1 14.0 %copy-start.11 = (f32[1584,768]{1,0:T(8,128)S(1)}, f32[1584,768]{1,0:T(8,128)}, u32[]{:S(2)}) copy-start(f32[1584,768]{1,0:T(8,128)} %reshape.370) | copy-start | bytes 14598148
  359.1 14.0 %copy-start.13 = (f32[1584,768]{1,0:T(8,128)S(1)}, f32[1584,768]{1,0:T(8,128)}, u32[]{:S(2)}) copy-start(f32[1584,768]{1,0:T(8,128)} %copy-done.12) | copy-start | bytes 14598148
  359.1 14.0 %copy-start.41 = (f32[768]{0:T(1024)S(1)}, f32[768]{0:T(1024)}, u32[]{:S(2)}) copy-start(f32[768]{0:T(1024)} %param.24) | copy-start | bytes 9220
  376.4 62.8 %copy-start.34 = (f32[768]{0:T(1024)S(1)}, f32[768]{0:T(1024)}, u32[]{:S(2)}) copy-start(f32[768]{0:T(1024)} %param.21) | copy-start | bytes 9220
  380.6 63.7 %copy-start.27 = (bf16[8,768]{1,0:T(8,128)(2,1)S(1)}, bf16[8,768]{1,0:T(8,128)(2,1)}, u32[]{:S(2)}) copy-start(bf16[8,768]{1,0:T(8,128)(2,1)} %reshape_squeeze.3) | copy-start | bytes 36868
  397.9 114.6 %reduce-scatter.24.cloned.1.call-start = ((), (), s32[]{:S(2)}) async-start(), calls=%async_computation.13 | async-start | bytes 1327104
  448.2 9.0 copy-start.26
  448.2 9.0 copy-start.32
  448.2 131.9 %reduce-scatter.18.cloned.1.call-start = ((), (), s32[]{:S(2)}) async-start(), calls=%async_computation.10 | async-start | bytes 1327104 | tf_op jit(solution)/shard_map/reduce_scatter | solution.py:281
  454.8 192.6 %reduce-scatter.14.cloned.1.call-start = ((), (), s32[]{:S(2)}) async-start(), calls=%async_computation.8 | async-start | bytes 1327104 | tf_op jit(solution)/shard_map/reduce_scatter | solution.py:272
  457.2 272.3 %reduce-scatter.16.cloned.1.call-start = ((), (), s32[]{:S(2)}) async-start(), calls=%async_computation.9 | async-start | bytes 3981312 | tf_op jit(solution)/shard_map/reduce_scatter | solution.py:278
  464.2 11.8 %copy-start.22 = (bf16[8,768]{1,0:T(8,128)(2,1)S(1)}, bf16[8,768]{1,0:T(8,128)(2,1)}, u32[]{:S(2)}) copy-start(bf16[8,768]{1,0:T(8,128)(2,1)} %copy-done.21) | copy-start | bytes 36868
  475.9 4.1 copy-start.47
  476.0 336.1 %reduce-scatter.12.cloned.1.call-start = ((), (), s32[]{:S(2)}) async-start(), calls=%async_computation.7 | async-start | bytes 3981312 | tf_op jit(solution)/shard_map/reduce_scatter | solution.py:269
  479.7 431.8 %reduce-scatter.20.cloned.1.call-start = ((), (), s32[]{:S(2)}) async-start(), calls=%async_computation.11 | async-start | bytes 5308416 | tf_op jit(solution)/shard_map/reduce_scatter | solution.py:287
  494.9 516.0 %reduce-scatter.22.cloned.1.call-start = ((), (), s32[]{:S(2)}) async-start(), calls=%async_computation.12 | async-start | bytes 5308416 | tf_op jit(solution)/shard_map/reduce_scatter | solution.py:290
  509.4 564.9 %all-reduce.15.cloned.1.call-start = ((), (), s32[]{:S(2)}) async-start(), calls=%async_computation.15 | async-start | bytes 5111808 | tf_op jit(solution)/shard_map/psum | solution.py:295
  1010.9 2.8 copy-start.49
  1014.3 4.0 copy-start.14
  1018.3 3.0 copy-start.44
  1018.3 37.1 %copy-start.29 = (bf16[8,768]{1,0:T(8,128)(2,1)S(1)}, bf16[8,768]{1,0:T(8,128)(2,1)}, u32[]{:S(2)}) copy-start(bf16[8,768]{1,0:T(8,128)(2,1)} %copy-done.28) | copy-start | bytes 36868
  1074.3 6.4 copy-start.19
  1074.3 7.4 copy-start.24
  1074.3 8.1 copy-start.23
  (9 other events, 7.0 us)
Sparse Core Ops, SparseCore 0:
  398.0 33.1 all-reduce.12
  448.3 64.1 reduce-scatter.23
  516.9 63.1 reduce-scatter.17
  584.3 62.9 reduce-scatter.13
  651.3 78.1 reduce-scatter.15
  733.3 78.6 reduce-scatter.11
  816.7 94.7 reduce-scatter.19
  915.6 95.1 reduce-scatter.21
  1014.5 59.6 all-reduce.14
where the time goes:
time: 1100 us; the launch traced here: 1090 us
  waiting for transfers between devices  536 us (49%)
  matrix products  236 us (21%)
  local copies, waits for them, and re-layouts  189 us (17%)
  other arithmetic  78.8 us (7%)
  blocking collectives  33.5 us (3%)
  between operations  16.2 us (1%)
    reduce_scatter x1, waiting for transfers between devices, on_device(): lax.psum_scatter(up_weight_grad.astype(jnp.bfloat16), 'video', scatter_di...  99.5 us
    reduce_scatter x1, waiting for transfers between devices, on_device(): lax.psum_scatter(down_weight_grad.astype(jnp.bfloat16), 'video', scatter_...  99.3 us
    reduce_scatter x1, waiting for transfers between devices, on_device(): lax.psum_scatter(mqkv_weight_grad.astype(jnp.bfloat16), 'video', scatter_...  82.6 us
    reduce_scatter x1, waiting for transfers between devices, on_device(): lax.psum_scatter(qkv_weight_grad.astype(jnp.bfloat16), 'video', scatter_d...  82.1 us
    reduce_scatter x1, waiting for transfers between devices, on_device(): lax.psum_scatter(message_out_weight_grad.astype(jnp.bfloat16), 'video', s...  67.2 us
    reduce_scatter x1, waiting for transfers between devices, on_device(): lax.psum_scatter(out_weight_grad.astype(jnp.bfloat16), 'video', scatter_d...  65.8 us
    dot_general x7, matrix products, dot_back(): lax.dot_general(left, right, (((1,), (1,)), ((), ())), preferred_element_...  62.8 us
    dot_general x8, matrix products, dot_plain(): return jnp.dot(left, right, preferred_element_type=jnp.float32)  56 us
  transfers between devices with their start and end apart: 9, of which 9 were waited for; matrix products, arithmetic and copies ran while one was open for 9% of the time, Pallas kernels for 0%

commit v1 on v0

v1 whole, which is shorter than its diff:
```python
import functools
import math

import jax
import jax.numpy as jnp
from jax import lax
from jax.experimental import pallas as pl
from jax.experimental.pallas import tpu as pltpu
from jax.sharding import PartitionSpec as P

H = 12
HD = 64
EPSILON = 1e-05
LOW = jnp.bfloat16
F32 = jnp.float32
BOTH = ("frame", "video")
SCALE = 1.0 / math.sqrt(HD)
PAIR = 2 * HD
PAIRS = H // 2
MESSAGE_TILE = 256
GAIN_ROWS = 16


def dot_nn(left, right):
    return lax.dot_general(
        left, right, (((1,), (0,)), ((), ())), preferred_element_type=F32
    )


def dot_nt(left, right):
    return lax.dot_general(
        left, right, (((1,), (1,)), ((), ())), preferred_element_type=F32
    )


def dot_tn(left, right):
    return lax.dot_general(
        left, right, (((0,), (0,)), ((), ())), preferred_element_type=F32
    )


def normalise(value):
    centred = value - jnp.mean(value, axis=-1, keepdims=True)
    inverse = lax.rsqrt(jnp.mean(centred * centred, axis=-1, keepdims=True) + EPSILON)
    return centred * inverse, inverse


def norm_back(upstream, normal, inverse, gain):
    scaled = upstream * gain
    inner = (
        scaled
        - jnp.mean(scaled, axis=-1, keepdims=True)
        - normal * jnp.mean(scaled * normal, axis=-1, keepdims=True)
    )
    return inner * inverse


def half_masks():
    first = lax.broadcasted_iota(jnp.int32, (1, PAIR), 1) < HD
    plain = (jnp.where(first, 1.0, 0.0).astype(LOW), jnp.where(first, 0.0, 1.0).astype(LOW))
    scaled = (jnp.where(first, SCALE, 0.0).astype(LOW), jnp.where(first, 0.0, SCALE).astype(LOW))
    return plain, scaled


def pair_forward(query, key, value, bias, masks):
    plain, scaled = masks
    context, logs = None, []
    for one, by in zip(plain, scaled):
        score = dot_nt(query * by, key) + bias
        top = jnp.max(score, axis=-1, keepdims=True)
        raised = jnp.exp(score - top)
        total = jnp.sum(raised, axis=-1, keepdims=True)
        prob_low = (raised * (1.0 / total)).astype(LOW)
        logs.append(top + jnp.log(total))
        part = dot_nn(prob_low, value * one)
        context = part if context is None else context + part
    return context, logs


def pair_backward(query, key, value, grad, logs, bias, masks):
    plain, scaled = masks
    query_grad = key_grad = value_grad = None
    for one, by, log in zip(plain, scaled, logs):
        query_by, grad_one, key_by = query * by, grad * one, key * by
        prob = jnp.exp(dot_nt(query_by, key) + bias - log)
        prob_grad = dot_nt(grad_one, value)
        inner = jnp.sum(prob * prob_grad, axis=-1, keepdims=True)
        score_low = (prob * (prob_grad - inner)).astype(LOW)
        parts = (
            dot_nn(score_low, key_by),
            dot_tn(score_low, query_by),
            dot_tn(prob.astype(LOW), grad_one),
        )
        if query_grad is None:
            query_grad, key_grad, value_grad = parts
        else:
            query_grad, key_grad, value_grad = (
                query_grad + parts[0],
                key_grad + parts[1],
                value_grad + parts[2],
            )
    return query_grad, key_grad, value_grad


def heads_forward(read, write, write_log, rows, width, bias):
    masks = half_masks()
    lane = lax.broadcasted_iota(jnp.int32, (rows, 128), 1)
    logs = jnp.zeros((rows, 128), F32)
    for pair in range(PAIRS):
        at = pair * PAIR
        context, pair_logs = pair_forward(
            read(at), read(width + at), read(2 * width + at), bias, masks
        )
        write(at, context.astype(LOW))
        for head in range(2):
            logs = jnp.where(lane == 2 * pair + head, pair_logs[head], logs)
    write_log(logs)


def heads_backward(read, read_grad, read_log, write, width, bias):
    masks = half_masks()
    for pair in range(PAIRS):
        at = pair * PAIR
        grads = pair_backward(
            read(at),
            read(width + at),
            read(2 * width + at),
            read_grad(at),
            (read_log(2 * pair), read_log(2 * pair + 1)),
            bias,
            masks,
        )
        for part in range(3):
            write(part * width + at, grads[part].astype(LOW))


def key_bias(tokens, padded):
    return jnp.where(lax.broadcasted_iota(jnp.int32, (1, padded), 1) < tokens, 0.0, -1e30)


def message_bias(flag, per_index, slots, videos):
    rows = flag.shape[0]
    row = lax.broadcasted_iota(jnp.int32, (rows, rows), 0)
    column = lax.broadcasted_iota(jnp.int32, (rows, rows), 1)
    same = (row // per_index == column // per_index) & (
        (row // slots) % videos == (column // slots) % videos
    )
    first = (lax.broadcasted_iota(jnp.int32, (rows, 128), 1) == 0).astype(LOW)
    alive = dot_nt(first, flag) > 0.5
    return jnp.where(same & alive, 0.0, -1e30)


WHOLE = pl.BlockSpec(memory_space=pltpu.VMEM)
SCALARS = pl.BlockSpec(memory_space=pltpu.SMEM)


def params(megabytes):
    return pltpu.CompilerParams(vmem_limit_bytes=megabytes << 20)


def cost(macs, moved, raised=0):
    return pl.CostEstimate(flops=2 * macs, bytes_accessed=moved, transcendentals=raised)


def shape(dims, dtype):
    return jax.ShapeDtypeStruct(dims, dtype)


def message_forward(sizes, payload, gain, proj, qkv, out):
    rows, wide = payload.shape
    width = proj.shape[0]
    tile = min(MESSAGE_TILE, rows)

    def body(pay, gain, proj, qkv, out, pre_o, low_o, qkv_o, log_o, context_o, two_o):
        pre = dot_nn(pay[:, :width], proj[...])
        pre_o[...] = pre
        normal, _ = normalise(pre)
        message = normal * gain[...]
        low = message.astype(LOW)
        low_o[...] = low
        qkv_o[...] = dot_nn(low, qkv[...]).astype(LOW)
        bias = message_bias(pay[:, width:], *sizes)

        def write(at, value):
            context_o[:, at : at + PAIR] = value

        def write_log(value):
            log_o[...] = value

        heads_forward(
            lambda at: qkv_o[:, at : at + PAIR], write, write_log, tile, width, bias
        )
        two_o[...] = message + dot_nn(context_o[...], out[...])

    def block(lanes):
        return pl.BlockSpec((tile, lanes), lambda i: (i, 0))

    return pl.pallas_call(
        body,
        grid=(rows // tile,),
        in_specs=[block(wide), WHOLE, WHOLE, WHOLE, WHOLE],
        out_specs=[block(width), block(width), block(3 * width), block(128), block(width), block(width)],
        out_shape=[
            shape((rows, width), F32),
            shape((rows, width), LOW),
            shape((rows, 3 * width), LOW),
            shape((rows, 128), F32),
            shape((rows, width), LOW),
            shape((rows, width), F32),
        ],
        compiler_params=params(48),
        cost_estimate=cost(5 * rows * width * width, 12 * width * width + 20 * rows * width),
        name="message_forward",
    )(payload, gain, proj, qkv, out)


def message_backward(
    sizes, ids, payload, two_low, pre, low, qkv_rows, logs, context, gain, proj, qkv, out, share
):
    rows, wide = payload.shape
    width = proj.shape[0]
    tile = min(MESSAGE_TILE, rows)

    def body(
        ids, pay, two, pre, low, rows_qkv, log, context, gain, proj, qkv, out,
        class_o, gain_o, proj_o, qkv_o, out_o, grad_s, triple_s,
    ):
        @pl.when(pl.program_id(0) == 0)
        def _():
            gain_o[...] = jnp.zeros_like(gain_o)
            proj_o[...] = jnp.zeros_like(proj_o)
            qkv_o[...] = jnp.zeros_like(qkv_o)
            out_o[...] = jnp.zeros_like(out_o)

        pick = lax.broadcasted_iota(jnp.int32, (width, share), 0) == (
            lax.broadcasted_iota(jnp.int32, (width, share), 1) + ids[1] * share
        )
        pick = jnp.where(pick, 1.0, 0.0).astype(LOW)
        two_rows = two[...]
        grad_s[...] = dot_nt(two_rows, out[...]).astype(LOW)
        out_o[...] += dot_tn(dot_nn(context[...], pick).astype(LOW), two_rows)
        bias = message_bias(pay[:, width:], *sizes)

        def write(at, value):
            triple_s[:, at : at + PAIR] = value

        heads_backward(
            lambda at: rows_qkv[:, at : at + PAIR],
            lambda at: grad_s[:, at : at + PAIR],
            lambda head: log[:, head : head + 1],
            write,
            width,
            bias,
        )
        triple = triple_s[...]
        qkv_o[...] += dot_tn(dot_nn(low[...], pick).astype(LOW), triple)
        upstream = two_rows.astype(F32) + dot_nt(triple, qkv[...])
        normal, inverse = normalise(pre[...])
        gain_o[...] += jnp.sum(upstream * normal, axis=0, keepdims=True)
        pre_low = norm_back(upstream, normal, inverse, gain[...]).astype(LOW)
        proj_o[...] += dot_tn(dot_nn(pay[:, :width], pick).astype(LOW), pre_low)
        class_o[...] = dot_nt(pre_low, proj[...])

    def block(lanes):
        return pl.BlockSpec((tile, lanes), lambda i: (i, 0))

    def fixed(dims):
        return pl.BlockSpec(dims, lambda i: (0, 0))

    return pl.pallas_call(
        body,
        grid=(rows // tile,),
        in_specs=[
            SCALARS, block(wide), block(width), block(width), block(width), block(3 * width),
            block(128), block(width), WHOLE, WHOLE, WHOLE, WHOLE,
        ],
        out_specs=[
            block(width), fixed((1, width)), fixed((share, width)), fixed((share, 3 * width)),
            fixed((share, width)),
        ],
        out_shape=[
            shape((rows, width), F32),
            shape((1, width), F32),
            shape((share, width), F32),
            shape((share, 3 * width), F32),
            shape((share, width), F32),
        ],
        scratch_shapes=[pltpu.VMEM((tile, width), LOW), pltpu.VMEM((tile, 3 * width), LOW)],
        compiler_params=params(48),
        cost_estimate=cost(8 * rows * width * width, 16 * width * width + 20 * rows * width),
        name="message_backward",
    )(ids, payload, two_low, pre, low, qkv_rows, logs, context, gain, proj, qkv, out)


def frame_forward(alive, tokens_in, cotangent, message, gain_one, gain_two, qkv, out, padded, step):
    videos, patches, slots, width = tokens_in.shape
    frames = videos * slots
    per = slots // step
    rows = step * padded

    def body(
        alive, tokens, grads, message, gain_one, gain_two, qkv, out,
        one_o, qkv_o, context_o, log_o, hidden_o, two_o, final_o, split_s, stream_s, grad_s,
    ):
        index = pl.program_id(0)
        video, part = index // per, index % per

        @pl.when(index == 0)
        def _():
            stream_s[...] = jnp.zeros_like(stream_s)
            grad_s[...] = jnp.zeros_like(grad_s)

        @pl.when(part == 0)
        def _():
            split_s[...] = tokens[0].astype(F32)
            for slot in range(slots):
                stream_s[slot, :patches, :] = split_s[:, slot, :]
                stream_s[slot, patches : patches + 1, :] = message[pl.ds(video * slots + slot, 1), :]
            split_s[...] = grads[0].astype(F32)
            for slot in range(slots):
                grad_s[:patches, :] = split_s[:, slot, :] * alive[video * slots + slot]
                final_o[slot] = grad_s[...].astype(LOW)

        stream = stream_s[pl.ds(part * step, step)].reshape(rows, width)
        one_low = (normalise(stream)[0] * gain_one[...]).astype(LOW)
        one_o[...] = one_low.reshape(step, padded, width)
        for third in range(3):
            cut = slice(third * width, (third + 1) * width)
            qkv_o[:, :, cut] = dot_nn(one_low, qkv[:, cut]).astype(LOW).reshape(step, padded, width)
        bias = key_bias(patches + 1, padded)
        for frame in range(step):

            def read(at):
                return qkv_o[frame, :, at : at + PAIR]

            def write(at, value):
                context_o[frame, :, at : at + PAIR] = value

            def write_log(value):
                log_o[frame] = value

            heads_forward(read, write, write_log, padded, width, bias)
        hidden = stream + dot_nn(context_o[...].reshape(rows, width), out[...])
        hidden_o[...] = hidden.reshape(step, padded, width)
        two_o[...] = (normalise(hidden)[0] * gain_two[...]).astype(LOW).reshape(step, padded, width)

    def block(lanes):
        return pl.BlockSpec((step, padded, lanes), lambda i: (i, 0, 0))

    per_video = pl.BlockSpec((1, patches, slots, width), lambda i: (i // per, 0, 0, 0))
    macs = 4 * frames * padded * width * width
    return pl.pallas_call(
        body,
        grid=(frames // step,),
        in_specs=[SCALARS, per_video, per_video, WHOLE, WHOLE, WHOLE, WHOLE, WHOLE],
        out_specs=[
            block(width), block(3 * width), block(width), block(128), block(width), block(width),
            pl.BlockSpec((slots, padded, width), lambda i: (i // per, 0, 0)),
        ],
        out_shape=[
            shape((frames, padded, width), LOW),
            shape((frames, padded, 3 * width), LOW),
            shape((frames, padded, width), LOW),
            shape((frames, padded, 128), F32),
            shape((frames, padded, width), F32),
            shape((frames, padded, width), LOW),
            shape((frames, padded, width), LOW),
        ],
        scratch_shapes=[
            pltpu.VMEM((patches, slots, width), F32),
            pltpu.VMEM((slots, padded, width), F32),
            pltpu.VMEM((padded, width), F32),
        ],
        compiler_params=params(58),
        cost_estimate=cost(2 * macs, 40 * frames * padded * width),
        name="frame_forward",
    )(alive, tokens_in, cotangent, message, gain_one, gain_two, qkv, out)


def slot_of(index, me, count):
    away = index ^ me
    return (away & 1) * (count // 2) + (away >> 1)


def store_shares(full, keep, send, core, place):
    half = full.shape[1] // 2
    left, right = full[:, :half].astype(LOW), full[:, half:].astype(LOW)
    first = core == 0
    place(keep, jnp.where(first, left, right))
    place(send, jnp.where(first, right, left))


def feed_forward(ids, alive, hidden, two, final, context, gain, up, down, dims, count):
    videos, patches, slots, padded = dims
    rows, width = hidden.shape
    inner = up.shape[1]
    blocks = inner // width
    half = width // 2
    frames = videos * slots
    tile = 2 * padded
    share, down_share = width // count, inner // count
    per_block = width // down_share
    low_count = per_block // 2

    def body(
        ids, alive, hidden, two, final, context, gain, up, down,
        encoded_o, grad_o, grad_low_o, up_keep, up_send, down_keep, down_send, out_keep, out_send, gain_o,
        total_s, act_s, back_s, join_s,
    ):
        step = pl.program_id(0)
        core, me = ids[0], ids[1]

        @pl.when(step == 0)
        def _():
            total_s[...] = hidden[...]
            grad_o[...] = jnp.zeros_like(grad_o)

        for part in range(rows // tile):
            cut = slice(part * tile, (part + 1) * tile)
            value = dot_nn(two[cut, :], up[...])
            act_grad = dot_nt(final[cut, :], down[...])
            sigma = 0.5 * jnp.tanh(0.851 * value) + 0.5
            act = value * sigma
            slope = sigma + 1.702 * (act - act * sigma)
            act_low = act.astype(LOW)
            back_low = (act_grad * slope).astype(LOW)
            act_s[cut, :] = act_low
            back_s[cut, :] = back_low
            total_s[cut, :] += dot_nn(act_low, down[...])
            grad_o[cut, :] += dot_nt(back_low, up[...])

        def place_rows(ref, value):
            for index in range(count):
                ref[slot_of(index, me, count), 0] = value[index * share : (index + 1) * share]

        def place_down(ref, value):
            for index in range(per_block):
                low = (index ^ me) & 1
                high = (index >> 1) ^ ((me >> 1) % low_count)
                ref[low, high] = value[index * down_share : (index + 1) * down_share]

        store_shares(dot_tn(two[...], back_s[...]), up_keep, up_send, core, place_rows)
        store_shares(dot_tn(act_s[...], final[...]), down_keep, down_send, core, place_down)

        @pl.when(step == blocks - 1)
        def _():
            gain_sum = jnp.zeros((1, width), F32)
            for video in range(videos):
                for slot in range(slots):
                    frame = video * slots + slot
                    cut = slice(frame * padded, (frame + 1) * padded)
                    join_s[:, slot, :] = total_s[cut, :][:patches] * alive[frame]
                    normal, inverse = normalise(hidden[cut, :])
                    upstream = grad_o[cut, :]
                    gain_sum += jnp.sum(upstream * normal, axis=0, keepdims=True)
                    back = norm_back(upstream, normal, inverse, gain[...])
                    back = final[cut, :].astype(F32) + back
                    grad_o[cut, :] = back
                    grad_low_o[cut, :] = back.astype(LOW)
                encoded_o[video] = join_s[...].astype(LOW)
            gain_o[...] = gain_sum
            store_shares(
                dot_tn(context[...], grad_low_o[...]), out_keep, out_send, core, place_rows
            )

    up_block = pl.BlockSpec((count, 1, share, half), lambda j, ids: (0, j, 0, 0))
    down_block = pl.BlockSpec(
        (2, low_count, down_share, half),
        lambda j, ids: (0, j ^ ((ids[1] >> 1) // low_count), 0, 0),
    )
    out_block = pl.BlockSpec((count, 1, share, half), lambda j, ids: (0, 0, 0, 0))
    up_shape = shape((count, blocks, share, half), LOW)
    down_shape = shape((2, count // 2, down_share, half), LOW)
    out_shape = shape((count, 1, share, half), LOW)
    return pl.pallas_call(
        body,
        grid_spec=pltpu.PrefetchScalarGridSpec(
            num_scalar_prefetch=1,
            grid=(blocks,),
            in_specs=[
                SCALARS, WHOLE, WHOLE, WHOLE, WHOLE, WHOLE,
                pl.BlockSpec((width, width), lambda j, ids: (0, j)),
                pl.BlockSpec((width, width), lambda j, ids: (j, 0)),
            ],
            out_specs=[
                WHOLE, WHOLE, WHOLE, up_block, up_block, down_block, down_block, out_block, out_block,
                WHOLE,
            ],
            scratch_shapes=[
                pltpu.VMEM((rows, width), F32),
                pltpu.VMEM((rows, width), LOW),
                pltpu.VMEM((rows, width), LOW),
                pltpu.VMEM((patches, slots, width), F32),
            ],
        ),
        out_shape=[
            shape((videos, patches, slots, width), LOW),
            shape((rows, width), F32),
            shape((rows, width), LOW),
            up_shape, up_shape, down_shape, down_shape, out_shape, out_shape,
            shape((1, width), F32),
        ],
        compiler_params=params(62),
        cost_estimate=cost(8 * rows * width * inner, 8 * width * inner + 20 * rows * width),
        name="feed_forward",
    )(ids, alive, hidden, two, final, context, gain, up, down)


def frame_backward(grad_low, qkv_rows, logs, out, tokens, step):
    frames, padded, width = grad_low.shape
    rows = step * padded

    def body(grad, rows_qkv, log, out, triple_o, context_s):
        context_s[...] = (
            dot_nt(grad[...].reshape(rows, width), out[...]).astype(LOW).reshape(step, padded, width)
        )
        bias = key_bias(tokens, padded)
        for frame in range(step):

            def write(at, value):
                triple_o[frame, :, at : at + PAIR] = value

            heads_backward(
                lambda at: rows_qkv[frame, :, at : at + PAIR],
                lambda at: context_s[frame, :, at : at + PAIR],
                lambda head: log[frame, :, head : head + 1],
                write,
                width,
                bias,
            )

    def block(lanes):
        return pl.BlockSpec((step, padded, lanes), lambda i: (i, 0, 0))

    return pl.pallas_call(
        body,
        grid=(frames // step,),
        in_specs=[block(width), block(3 * width), block(128), WHOLE],
        out_specs=block(3 * width),
        out_shape=shape((frames, padded, 3 * width), LOW),
        scratch_shapes=[pltpu.VMEM((step, padded, width), LOW)],
        compiler_params=params(56),
        cost_estimate=cost(22 * frames * padded * width * width // 4, 16 * frames * padded * width),
        name="frame_backward",
    )(grad_low, qkv_rows, logs, out)


def qkv_weight_grad(ids, one, triple, count):
    rows, width = one.shape
    blocks = triple.shape[1] // width
    share, half = width // count, width // 2

    def body(ids, one, triple, keep, send):
        me = ids[1]

        def place_rows(ref, value):
            for index in range(count):
                ref[slot_of(index, me, count), 0] = value[index * share : (index + 1) * share]

        store_shares(dot_tn(one[...], triple[...]), keep, send, ids[0], place_rows)

    block = pl.BlockSpec((count, 1, share, half), lambda j: (0, j, 0, 0))
    out = shape((count, blocks, share, half), LOW)
    return pl.pallas_call(
        body,
        grid=(blocks,),
        in_specs=[SCALARS, WHOLE, pl.BlockSpec((rows, width), lambda j: (0, j))],
        out_specs=[block, block],
        out_shape=[out, out],
        compiler_params=params(48),
        cost_estimate=cost(3 * rows * width * width, 8 * rows * width + 6 * width * width),
        name="qkv_weight_grad",
    )(ids, one, triple)


def stream_backward(tokens_in, message, grad, triple, gain, qkv, feed_gain, step):
    videos, patches, slots, width = tokens_in.shape
    frames, padded, _ = grad.shape
    per = slots // step
    rows = step * padded

    def body(
        tokens, message, grad, triple, gain, qkv, feed_gain, stream_o, message_o,
        split_s, stream_s, back_s, row_s, gain_s,
    ):
        index = pl.program_id(0)
        video, part = index // per, index % per

        @pl.when(index == 0)
        def _():
            stream_s[...] = jnp.zeros_like(stream_s)
            row_s[...] = jnp.zeros_like(row_s)
            gain_s[...] = jnp.zeros_like(gain_s)

        @pl.when(part == 0)
        def _():
            split_s[...] = tokens[0].astype(F32)
            for slot in range(slots):
                stream_s[slot, :patches, :] = split_s[:, slot, :]
                stream_s[slot, patches : patches + 1, :] = message[pl.ds(video * slots + slot, 1), :]

        upstream = dot_nt(triple[...].reshape(rows, 3 * width), qkv[...])
        normal, inverse = normalise(stream_s[pl.ds(part * step, step)].reshape(rows, width))
        gain_s[...] += jnp.sum(upstream * normal, axis=0, keepdims=True)
        back = norm_back(upstream, normal, inverse, gain[...]).reshape(step, padded, width)
        back = grad[...] + back
        back_s[pl.ds(part * step, step)] = back
        for frame in range(step):
            row_s[pl.ds(index * step + frame, 1), :] = back[frame, patches : patches + 1, :]

        @pl.when(part == per - 1)
        def _():
            for slot in range(slots):
                stream_o[0, :, slot, :] = back_s[slot, :patches, :]

        @pl.when(index == frames // step - 1)
        def _():
            row_s[frames : frames + 1, :] = gain_s[...]
            row_s[frames + 1 : frames + 2, :] = feed_gain[...]
            message_o[...] = row_s[...].astype(LOW)

    def block(lanes):
        return pl.BlockSpec((step, padded, lanes), lambda i: (i, 0, 0))

    per_video = pl.BlockSpec((1, patches, slots, width), lambda i: (i // per, 0, 0, 0))
    return pl.pallas_call(
        body,
        grid=(frames // step,),
        in_specs=[per_video, WHOLE, block(width), block(3 * width), WHOLE, WHOLE, WHOLE],
        out_specs=[per_video, pl.BlockSpec((GAIN_ROWS, width), lambda i: (0, 0))],
        out_shape=[shape((videos, patches, slots, width), F32), shape((GAIN_ROWS, width), LOW)],
        scratch_shapes=[
            pltpu.VMEM((patches, slots, width), F32),
            pltpu.VMEM((slots, padded, width), F32),
            pltpu.VMEM((slots, padded, width), F32),
            pltpu.VMEM((GAIN_ROWS, width), F32),
            pltpu.VMEM((1, width), F32),
        ],
        compiler_params=params(56),
        cost_estimate=cost(3 * frames * padded * width * width, 16 * frames * padded * width),
        name="stream_backward",
    )(tokens_in, message, grad, triple, gain, qkv, feed_gain)


def swap(value, frame_bits, video_bits):
    frames, videos = lax.axis_size("frame"), lax.axis_size("video")
    pairs = [
        (f * videos + v, (f ^ frame_bits) * videos + (v ^ video_bits))
        for f in range(frames)
        for v in range(videos)
    ]
    return lax.ppermute(value, BOTH, pairs)


def gather_all(value):
    frames, videos = lax.axis_size("frame"), lax.axis_size("video")
    value = jnp.stack([value] + [swap(value, 0, 2 * z) for z in range(1, videos // 2)], axis=0)
    value = jnp.stack([value] + [swap(value, 2 * y, 0) for y in range(1, frames // 2)], axis=1)
    value = jnp.stack([value, swap(value, 0, 1)], axis=0)
    value = jnp.stack([value, swap(value, 1, 0)], axis=2)
    return value.reshape(videos, frames, *value.shape[4:])


def reduce_shares(keep, send):
    frames, videos = lax.axis_size("frame"), lax.axis_size("video")
    half = videos // 2
    core = lax.axis_index("frame") & 1
    got = [swap(s, 1, 0) for s in send]

    def first(k, g, cut):
        return k[cut].astype(F32) + g[cut].astype(F32)

    out = [first(k, g, slice(half, None)).astype(LOW) for k, g in zip(keep, got)]
    across = [swap(o, 0, 1) for o in out]
    total = []
    for k, g, a in zip(keep, got, across):
        near = [first(k, g, slice(z, z + 1)) + a[z : z + 1].astype(F32) for z in range(half)]
        parts = [swap(near[z].astype(LOW), 0, 2 * z) for z in range(1, half)]
        summed = near[0]
        for part in parts:
            summed = summed + part.astype(F32)
        total.append(summed[0].astype(LOW))
    bit = 2
    while bit < frames:
        total = lax.optimization_barrier(total)
        total = [(t.astype(F32) + swap(t, bit, 0).astype(F32)).astype(LOW) for t in total]
        bit *= 2
    total = lax.optimization_barrier(total)
    other = [swap(t, 1, 0) for t in total]
    result = []
    for mine, theirs in zip(total, other):
        left = jnp.where(core == 0, mine, theirs)
        right = jnp.where(core == 0, theirs, mine)
        both = jnp.stack([left, right], axis=2)
        blocks, share, _, columns = both.shape
        both = both.transpose(1, 0, 2, 3).reshape(share, blocks * 2 * columns)
        result.append(both.astype(F32))
    return result


def on_device(
    frames,
    out_cotangent,
    frame_counts,
    message_proj,
    message_gain,
    message_qkv,
    message_out,
    attn_gain,
    attn_qkv,
    attn_out,
    mlp_gain,
    mlp_up,
    mlp_down,
):
    videos, slots, patches, width = frames.shape
    tokens = patches + 1
    padded = -(-tokens // 16) * 16
    frame_total = videos * slots
    row_total = frame_total * padded
    frame_axis, video_axis = lax.axis_size("frame"), lax.axis_size("video")
    frame_index, video_index = lax.axis_index("frame"), lax.axis_index("video")
    share = width // video_axis
    ids = jnp.stack([frame_index & 1, video_index]).astype(jnp.int32)
    slot_ids = frame_index * slots + jnp.arange(slots, dtype=jnp.int32)
    alive = (slot_ids[None, :] < frame_counts[:, None]).astype(F32).reshape(frame_total)
    gains = [g.reshape(1, width) for g in (message_gain, attn_gain, mlp_gain)]
    tokens_in = frames.transpose(0, 2, 1, 3)
    cotangent = out_cotangent.transpose(0, 2, 1, 3)

    class_rows = tokens_in[:, 0].reshape(frame_total, width)
    flags = jnp.broadcast_to(alive.astype(LOW)[:, None], (frame_total, 128))
    sizes = (frame_axis * frame_total, slots, videos)
    payload = gather_all(jnp.concatenate([class_rows, flags], axis=1))
    payload = payload.reshape(-1, width + 128)
    pre, low, qkv_rows, message_logs, mcontext, message_two = message_forward(
        sizes, payload, gains[0], message_proj, message_qkv, message_out
    )
    message_two = message_two[:frame_total]

    step = min(2, slots)
    one, triple, context, logs, hidden, two, final = frame_forward(
        alive, tokens_in, cotangent, message_two, gains[1], gains[2], attn_qkv, attn_out, padded, step
    )
    (
        encoded, hidden_grad, hidden_low, up_keep, up_send, down_keep, down_send, out_keep, out_send,
        feed_gain,
    ) = feed_forward(
        ids,
        alive,
        hidden.reshape(row_total, width),
        two.reshape(row_total, width),
        final.reshape(row_total, width),
        context.reshape(row_total, width),
        gains[2],
        mlp_up,
        mlp_down,
        (videos, patches, slots, padded),
        video_axis,
    )
    down_keep, down_send = (
        a.reshape(video_axis, 1, *a.shape[2:]) for a in (down_keep, down_send)
    )
    up_sum, down_sum, out_sum = reduce_shares(
        [up_keep, down_keep, out_keep], [up_send, down_send, out_send]
    )

    triple_grad = frame_backward(
        hidden_low.reshape(frame_total, padded, width), triple, logs, attn_out, tokens, step
    )
    qkv_keep, qkv_send = qkv_weight_grad(
        ids, one.reshape(row_total, width), triple_grad.reshape(row_total, 3 * width), video_axis
    )
    (qkv_sum,) = reduce_shares([qkv_keep], [qkv_send])
    stream_grad, rows_out = stream_backward(
        tokens_in,
        message_two,
        hidden_grad.reshape(frame_total, padded, width),
        triple_grad,
        gains[1],
        attn_qkv,
        feed_gain,
        step,
    )
    rows_all = gather_all(rows_out)
    two_low = rows_all[:, :, :frame_total].reshape(-1, width)
    gain_sums = rows_all[:, :, frame_total : frame_total + 2].astype(F32).sum(axis=(0, 1))
    class_grad, message_gain_grad, proj_sum, mqkv_sum, message_out_sum = message_backward(
        sizes, ids, payload, two_low, pre, low, qkv_rows, message_logs, mcontext,
        gains[0], message_proj, message_qkv, message_out, share,
    )
    class_grad = class_grad[:frame_total].reshape(videos, 1, slots, width)
    stream_grad = lax.dynamic_update_slice(
        stream_grad, stream_grad[:, :1] + class_grad, (0, 0, 0, 0)
    )
    cut = video_index * share
    message_gain_sum = lax.dynamic_slice(message_gain_grad[0], (cut,), (share,))
    attn_gain_sum = lax.dynamic_slice(gain_sums[0], (cut,), (share,))
    mlp_gain_sum = lax.dynamic_slice(gain_sums[1], (cut,), (share,))
    return (
        encoded.transpose(0, 2, 1, 3),
        stream_grad.transpose(0, 2, 1, 3),
        proj_sum,
        message_gain_sum,
        mqkv_sum,
        message_out_sum,
        attn_gain_sum,
        qkv_sum,
        out_sum,
        mlp_gain_sum,
        up_sum,
        down_sum,
    )


def solution(mesh):
    return jax.shard_map(
        on_device,
        mesh=mesh,
        in_specs=(
            P("video", "frame", None, None),
            P("video", "frame", None, None),
            P("video"),
            P(),
            P(),
            P(),
            P(),
            P(),
            P(),
            P(),
            P(),
            P(),
            P(),
        ),
        out_specs=(
            P("video", "frame", None, None),
            P("video", "frame", None, None),
            P("video", None),
            P("video"),
            P("video", None),
            P("video", None),
            P("video"),
            P("video", None),
            P("video", None),
            P("video"),
            P("video", None),
            P("video", None),
        ),
        check_vma=False,
    )
```

time: 1100 us -> 374 us (0.34)
  waiting for transfers between devices: 536 us -> 104 us
  matrix products: 236 us -> 0 us
  Pallas kernels: 0 us -> 179 us
  local copies, waits for them, and re-layouts: 189 us -> 19.5 us
  other arithmetic: 78.8 us -> 24.4 us
  starting transfers between devices: 1.13 us -> 40.6 us
  blocking collectives: 33.5 us -> 0 us
  between operations: 16.2 us -> 1.35 us
    reduce_scatter x6 -> x0, waiting for transfers between devices: 497 us -> none  [the longest x1 99.5 us: on_device(): lax.psum_scatter(up_weight_grad.astype(jnp.bfloat16), 'video', scatter_di...]
    dot_general x42 -> x0, matrix products: 236 us -> none  [the longest x7 62.8 us: dot_back(): lax.dot_general(left, right, (((1,), (1,)), ((), ())), preferred_element_...]
    pallas_call x0 -> x7, Pallas kernels: none -> 179 us  [the longest x1 70.5 us: feed_forward(): pl.pallas_call(body, grid_spec=pltpu.PrefetchScalarGridSpec(num_scalar_pr...]
    ppermute x0 -> x40, waiting for transfers between devices: none -> 104 us  [swap(): return lax.ppermute(value, BOTH, pairs)]
    reshape x17 -> x4, local copies, waits for them, and re-layouts: 80.1 us -> 3.25 us  [the longest x3 3.24 us: on_device(): gains = [g.reshape(1, width) for g in (message_gain, attn_gain, mlp_gain)]]
    ppermute x0 -> x40, starting transfers between devices: none -> 40.6 us  [swap(): return lax.ppermute(value, BOTH, pairs)]
    unnamed x11 -> x0, waiting for transfers between devices: 29.7 us -> none
    convert_element_type x16 -> x22, other arithmetic: 41.6 us -> 18.3 us  [the longest x4 6.96 us: reduce_shares(): first(k, g, slice(half, None)).astype(LOW)]
  transfers between devices with their start and end apart: 9 -> 40, of which waited for: 9 -> 20; matrix products, arithmetic and copies ran while one was open for 9% -> 9% of each run, Pallas kernels for 0% -> 6%
where the time goes in v1:
time: 374 us; the launch traced here: 369 us
  Pallas kernels  179 us (48%)
  waiting for transfers between devices  104 us (28%)
  starting transfers between devices  40.6 us (11%)
  other arithmetic  24.4 us (7%)
  local copies, waits for them, and re-layouts  19.5 us (5%)
    ppermute x40, waiting for transfers between devices, swap(): return lax.ppermute(value, BOTH, pairs)  104 us
    pallas_call x1, Pallas kernels, feed_forward(): pl.pallas_call(body, grid_spec=pltpu.PrefetchScalarGridSpec(num_scalar_pr...  70.5 us
    ppermute x40, starting transfers between devices, swap(): return lax.ppermute(value, BOTH, pairs)  40.6 us
    pallas_call x1, Pallas kernels, frame_backward(): pl.pallas_call(body, grid=(frames // step,), in_specs=[block(width), bloc...  32.9 us
    pallas_call x1, Pallas kernels, frame_forward(): pl.pallas_call(body, grid=(frames // step,), in_specs=[SCALARS, per_video...  31.8 us
    pallas_call x1, Pallas kernels, stream_backward(): pl.pallas_call(body, grid=(frames // step,), in_specs=[per_video, WHOLE,...  16.4 us
    pallas_call x1, Pallas kernels, message_backward(): pl.pallas_call(body, grid=(rows // tile,), in_specs=[SCALARS, block(wide)...  10.3 us
    pallas_call x1, Pallas kernels, qkv_weight_grad(): pl.pallas_call(body, grid=(blocks,), in_specs=[SCALARS, WHOLE, pl.BlockSp...  10.1 us
  transfers between devices with their start and end apart: 40, of which 20 were waited for; matrix products, arithmetic and copies ran while one was open for 9% of the time, Pallas kernels for 6%

profile of v1, /device:TPU:0, one launch (start us, length us, event | category | flops | bytes accessed | tf_op | source)
XLA Modules:
  0.0 369.0 jit_solution(3692050765254769359)
XLA Ops:
  2.4 4.0 %collective-permute-start.1 = (bf16[8,896]{1,0:T(8,128)(2,1)S(1)}, bf16[8,896]{1,0:T(8,128)(2,1)S(1)}, u32[]{:S(2)}, u32[]{:S(2)}) collective-permute-start(bf16[8,896]{1,0:T(8,128)(2,1)S(1)} %get-tuple-element.133), channel_id=1, source_target_pairs={{0,4},{1,5},{2,6},{3,7},{4,0},{5,1},{6,2},{7,3},{8,12},{9,13},{10,... | collective-permute-start | bytes 43016 | tf_op jit(solution)/shard_map/ppermute | solution.py:652
  6.4 1.6 collective-permute-start
  8.1 2.0 collective-permute-done
  10.1 3.4 collective-permute-done.2
  13.5 1.6 collective-permute-start.3
  15.1 2.7 collective-permute-done.3
  17.8 1.6 collective-permute-start.4
  19.4 3.3 collective-permute-done.4
  23.5 1.3 reshape.151.gain_one.gain
  24.8 1.3 reshape.152.gain_two.gain
  26.7 7.3 %message_forward.1 = (f32[256,768]{1,0:T(8,128)S(1)}, bf16[256,768]{1,0:T(8,128)(2,1)S(1)}, bf16[256,2304]{1,0:T(8,128)(2,1)S(1)}, f32[256,128]{1,0:T(8,128)S(1)...) custom-call(bf16[256,896]{1,0:T(8,128)(2,1)S(1)} %bitcast.95, f32[1,768]{1,0:T(1,128)S(1)} %reshape.150.gain, ...), custom_call_target="tpu_custom_call" | custom-call | flops 1509949440 | bytes 11010048 | tf_op jit(solution)/shard_map/message_forward/pallas_call | solution.py:198
  34.0 1.0 copy-done.3
  37.9 31.8 %frame_forward.1 = (bf16[8,208,768]{2,1,0:T(8,128)(2,1)}, bf16[8,208,2304]{2,1,0:T(8,128)(2,1)}, bf16[8,208,768]{2,1,0:T(8,128)(2,1)}, f32[8,208,128]{2,1,0:T(8,...) custom-call(f32[8]{0:T(128)} %copy-done.20, ...), custom_call_target="tpu_custom_call" | custom-call | flops 15703474176 | bytes 51118080 | tf_op jit(solution)/shard_map/frame_forward/pallas_call | solution.py:352
  69.7 70.5 %feed_forward.1 = (bf16[2,197,4,768]{3,2,1,0:T(4,128)(2,1)}, f32[1664,768]{1,0:T(8,128)}, bf16[1664,768]{1,0:T(8,128)(2,1)}, bf16[8,4,96,384]{3,2,1,0:T(8,128)(2...) custom-call(s32[2]{0:T(128)} %pad_add_fusion.ids, ...), custom_call_target="tpu_custom_call" | custom-call | flops 62813896704 | bytes 44433408 | tf_op jit(solution)/shard_map/feed_forward/pallas_call | solution.py:475
  140.1 32.9 %frame_backward.1.triple = bf16[8,208,2304]{2,1,0:T(8,128)(2,1)} custom-call(bf16[8,208,768]{2,1,0:T(8,128)(2,1)} %bitcast.129, bf16[8,208,2304]{2,1,0:T(8,128)(2,1)} %get-tuple-element.58.rows_qkv, f32[8,208,128]{2,1,0:T(8,128)} %get-tuple-element.59.log, bf16[768,768]{1,0:T(8,128)(2,1)} %out.6), custom_call_target="tpu_custom_call" | custom-call | flops 10796138496 | bytes 20447232 | tf_op jit(solution)/shard_map/frame_backward/pallas_call | solution.py:535
  173.1 16.4 %stream_backward.1 = (f32[2,197,4,768]{3,2,1,0:T(4,128)}, bf16[16,768]{1,0:T(8,128)(2,1)}) custom-call(bf16[2,197,4,768]{3,2,1,0:T(4,128)(2,1)} %bitcast.121, f32[8,768]{1,0:T(8,128)} %slice.194.message, f32[8,208,768]{2,1,0:T(8,128)} %bitcast.124, bf16[8,208,2304]{2,1,0:T(8,128)(2,1)} %frame_backward.1.triple, f32[1,768]{1,0:T(1,128)} %reshape.151.gain_one.gain, ...), custom_call_target="tpu_custom_call" | custom-call | flops 5888802816 | bytes 20447232 | tf_op jit(solution)/shard_map/stream_backward/pallas_call | solution.py:626
  189.6 4.2 %collective-permute-start.6 = (bf16[16,768]{1,0:T(8,128)(2,1)}, bf16[16,768]{1,0:T(8,128)(2,1)S(1)}, u32[]{:S(2)}, u32[]{:S(2)}) collective-permute-start(bf16[16,768]{1,0:T(8,128)(2,1)} %get-tuple-element.62), channel_id=1, source_target_pairs={{0,2},{1,3},{2,0},{3,1},{4,6},{5,7},{6,4},{7,5},{8,10},{9,11},{10,... | collective-permute-start | bytes 73736 | tf_op jit(solution)/shard_map/ppermute | solution.py:652
  194.3 1.1 collective-permute-done.8
  196.6 1.6 collective-permute-start.9
  198.2 10.1 %qkv_weight_grad.1 = (bf16[8,3,96,384]{3,2,1,0:T(8,128)(2,1)S(1)}, bf16[8,3,96,384]{3,2,1,0:T(8,128)(2,1)}) custom-call(s32[2]{0:T(128)S(1)} %copy-done.13, bf16[1664,768]{1,0:T(8,128)(2,1)S(1)} %bitcast.98, bf16[1664,2304]{1,0:T(8,128)(2,1)} %bitcast.123), custom_call_target="tpu_custom_call" | custom-call | flops 5888802816 | bytes 13762560 | tf_op jit(solution)/shard_map/qkv_weight_grad/pallas_call | solution.py:564
  208.4 1.2 copy-done.1
  209.6 1.6 collective-permute-start.10
  211.4 5.6 %collective-permute-done.10 = bf16[4,2,16,768]{3,2,0,1:T(8,128)(2,1)S(1)} collective-permute-done((bf16[4,2,16,768]{3,2,0,1:T(8,128)(2,1)S(1)}, bf16[4,2,16,768]{3,2,0,1:T(8,128)(2,1)S(1)}, u32[]{:S(2)}, u32[]{:S(2)}) %collective-permute-start.10) | collective-permute-done | bytes 196640 | tf_op jit(solution)/shard_map/ppermute | solution.py:652
  217.9 1.9 add_convert_fusion.4
  219.8 1.5 collective-permute-start.30
  221.3 1.1 pad_maximum_fusion
  223.3 10.3 %message_backward.1 = (f32[256,768]{1,0:T(8,128)S(1)}, f32[1,768]{1,0:T(1,128)S(1)}, f32[96,768]{1,0:T(8,128)}, f32[96,2304]{1,0:T(8,128)}, f32[96,768]{1,0:T(8,128)}) custom-call(s32[2]{0:T(128)S(1)} %copy-done.13, bf16[256,896]{1,0:T(8,128)(2,1)S(1)} %bitcast.96, bf16[256,768]{1,0:T(8,128)(2,1)S(1)} %bitcast.97, f32[256,768]{1,0:T(8,128)S(1)} %copy-done.6, ...), custom_call_target="tpu_custom_call" | custom-call | flops 2415919104 | bytes 13369344 | tf_op jit(solution)/shard_map/message_backward/pallas_call | solution.py:270
  233.6 1.2 convert_reduce_fusion
  234.9 1.4 fusion.5
  236.2 1.7 add_convert_fusion.1
  238.5 1.8 add_convert_fusion
  240.4 1.3 collective-permute-start.20
  241.7 1.2 add_convert_fusion.22
  242.8 2.1 collective-permute-start.31
  244.9 1.6 fusion
  248.3 1.1 collective-permute-start.32
  250.0 4.1 %collective-permute-done.33 = bf16[1,1,96,384]{3,2,1,0:T(8,128)(2,1)S(1)} collective-permute-done((bf16[1,1,96,384]{3,2,1,0:T(8,128)(2,1)S(1)}, bf16[1,1,96,384]{3,2,1,0:T(8,128)(2,1)S(1)}, u32[]{:S(2)}, u32[]{:S(2)}) %collective-permute-start.33) | collective-permute-done | bytes 73760 | tf_op jit(solution)/shard_map/ppermute | solution.py:652
  254.1 2.3 collective-permute-done.32
  257.3 3.1 collective-permute-done.13
  260.5 1.4 add_convert_fusion.17
  261.9 2.0 collective-permute-start.14
  264.4 1.1 collective-permute-start.15
  265.5 20.3 %collective-permute-done.20 = bf16[4,4,96,384]{3,2,1,0:T(8,128)(2,1)S(1)} collective-permute-done((bf16[4,4,96,384]{3,2,1,0:T(8,128)(2,1)S(1)}, bf16[4,4,96,384]{3,2,1,0:T(8,128)(2,1)S(1)}, u32[]{:S(2)}, u32[]{:S(2)}) %collective-permute-start.20) | collective-permute-done | bytes 1179680 | tf_op jit(solution)/shard_map/ppermute | solution.py:652
  285.7 1.5 add_convert_fusion.12
  287.2 2.0 collective-permute-start.21
  289.3 1.1 fusion.3
  291.3 1.1 collective-permute-start.22
  292.5 17.8 %collective-permute-done.25 = bf16[4,1,384,384]{3,2,0,1:T(8,128)(2,1)S(1)} collective-permute-done((bf16[4,1,384,384]{3,2,0,1:T(8,128)(2,1)S(1)}, bf16[4,1,384,384]{3,2,0,1:T(8,128)(2,1)S(1)}, u32[]{:S(2)}, u32[]{:S(2)}) %collective-permute-start.25) | collective-permute-done | bytes 1179680 | tf_op jit(solution)/shard_map/ppermute | solution.py:652
  310.3 1.5 add_convert_fusion.8
  311.8 2.1 collective-permute-start.26
  314.3 1.1 collective-permute-start.27
  315.6 2.4 collective-permute-done.22
  318.0 1.2 fusion.1
  319.1 10.2 %collective-permute-done.26 = bf16[1,1,384,384]{3,2,0,1:T(8,128)(2,1)S(1)} collective-permute-done((bf16[1,1,384,384]{3,2,0,1:T(8,128)(2,1)S(1)}, bf16[1,1,384,384]{3,2,0,1:T(8,128)(2,1)S(1)}, u32[]{:S(2)}, u32[]{:S(2)}) %collective-permute-start.26) | collective-permute-done | bytes 294944 | tf_op jit(solution)/shard_map/ppermute | solution.py:652
  329.3 12.6 %collective-permute-done.27 = bf16[1,1,384,384]{3,2,0,1:T(8,128)(2,1)S(1)} collective-permute-done((bf16[1,1,384,384]{3,2,0,1:T(8,128)(2,1)S(1)}, bf16[1,1,384,384]{3,2,0,1:T(8,128)(2,1)S(1)}, u32[]{:S(2)}, u32[]{:S(2)}) %collective-permute-start.27) | collective-permute-done | bytes 294944 | tf_op jit(solution)/shard_map/ppermute | solution.py:652
  342.0 1.2 fusion.2
  343.2 1.6 collective-permute-start.36
  345.3 1.6 collective-permute-start.35
  346.9 1.5 collective-permute-done.36
  348.5 6.3 %collective-permute-done.34 = bf16[4,96,384]{2,1,0:T(8,128)(2,1)S(1)} collective-permute-done((bf16[4,96,384]{2,1,0:T(8,128)(2,1)S(1)}, bf16[4,96,384]{2,1,0:T(8,128)(2,1)S(1)}, u32[]{:S(2)}, u32[]{:S(2)}) %collective-permute-start.34) | collective-permute-done | bytes 294944 | tf_op jit(solution)/shard_map/ppermute | solution.py:652
  354.8 4.1 %collective-permute-done.35 = bf16[1,384,384]{2,1,0:T(8,128)(2,1)S(1)} collective-permute-done((bf16[1,384,384]{2,1,0:T(8,128)(2,1)S(1)}, bf16[1,384,384]{2,1,0:T(8,128)(2,1)S(1)}, u32[]{:S(2)}, u32[]{:S(2)}) %collective-permute-start.35) | collective-permute-done | bytes 294944 | tf_op jit(solution)/shard_map/ppermute | solution.py:652
  360.1 1.6 reshape.167
  364.3 1.4 copy.36
  366.8 2.0 reshape.170
  (127 shorter events, 21.5 us)
Async XLA Ops:
  0.6 26.0 %copy-start = (bf16[768,768]{1,0:T(8,128)(2,1)S(1)}, bf16[768,768]{1,0:T(8,128)(2,1)}, u32[]{:S(2)}) copy-start(bf16[768,768]{1,0:T(8,128)(2,1)} %proj.3) | copy-start | bytes 3538948
  1.6 32.4 %copy-start.20 = (f32[8]{0:T(128)}, f32[8]{0:T(128)S(1)}, u32[]{:S(2)}) copy-start(f32[8]{0:T(128)S(1)} %reshape.166.alive) | copy-start | bytes 100
  2.4 5.7 %collective-permute-start.1 = (bf16[8,896]{1,0:T(8,128)(2,1)S(1)}, bf16[8,896]{1,0:T(8,128)(2,1)S(1)}, u32[]{:S(2)}, u32[]{:S(2)}) collective-permute-start(bf16[8,896]{1,0:T(8,128)(2,1)S(1)} %get-tuple-element.133), channel_id=1, source_target_pairs={{0,4},{1,5},{2,6},{3,7},{4,0},{5,1},{6,2},{7,3},{8,12},{9,13},{10,... | collective-permute-start | bytes 43016 | tf_op jit(solution)/shard_map/ppermute | solution.py:652
  6.4 3.7 %collective-permute-start = (bf16[8,896]{1,0:T(8,128)(2,1)S(1)}, bf16[8,896]{1,0:T(8,128)(2,1)S(1)}, u32[]{:S(2)}, u32[]{:S(2)}) collective-permute-start(bf16[8,896]{1,0:T(8,128)(2,1)S(1)} %get-tuple-element.133), channel_id=1, source_target_pairs={{0,2},{1,3},{2,0},{3,1},{4,6},{5,7},{6,4},{7,5},{8,10},{9,11},{10,... | collective-permute-start | bytes 43016 | tf_op jit(solution)/shard_map/ppermute | solution.py:652
  8.0 5.5 %collective-permute-start.2 = (bf16[8,896]{1,0:T(8,128)(2,1)S(1)}, bf16[8,896]{1,0:T(8,128)(2,1)S(1)}, u32[]{:S(2)}, u32[]{:S(2)}) collective-permute-start(bf16[8,896]{1,0:T(8,128)(2,1)S(1)} %get-tuple-element.133), channel_id=1, source_target_pairs={{0,6},{1,7},{2,4},{3,5},{4,2},{5,3},{6,0},{7,1},{8,14},{9,15},{10,... | collective-permute-start | bytes 43016 | tf_op jit(solution)/shard_map/ppermute | solution.py:652
  13.5 4.2 %collective-permute-start.3 = (bf16[4,8,896]{2,1,0:T(8,128)(2,1)S(1)}, bf16[4,8,896]{2,1,0:T(8,128)(2,1)S(1)}, u32[]{:S(2)}, u32[]{:S(2)}) collective-permute-start(bf16[4,8,896]{2,1,0:T(8,128)(2,1)S(1)} %get-tuple-element.131), channel_id=1, source_target_pairs={{0,16},{1,17},{2,18},{3,19},{4,20},{5,21},{6,22},{7,23},{8,24},{9,... | collective-permute-start | bytes 172040 | tf_op jit(solution)/shard_map/ppermute | solution.py:652
  17.8 4.9 %collective-permute-start.4 = (bf16[4,2,8,896]{3,2,1,0:T(8,128)(2,1)S(1)}, bf16[4,2,8,896]{3,2,1,0:T(8,128)(2,1)S(1)}, u32[]{:S(2)}, u32[]{:S(2)}) collective-permute-start(bf16[4,2,8,896]{3,2,1,0:T(8,128)(2,1)S(1)} %get-tuple-element.127), channel_id=1, source_target_pairs={{0,1},{1,0},{2,3},{3,2},{4,5},{5,4},{6,7},{7,6},{8,9},{9,8},{10,11... | collective-permute-start | bytes 344072 | tf_op jit(solution)/shard_map/ppermute | solution.py:652
  22.7 3.9 %collective-permute-start.5 = (bf16[2,4,2,8,896]{4,3,2,1,0:T(8,128)(2,1)S(1)}, bf16[2,4,2,8,896]{4,3,2,1,0:T(8,128)(2,1)S(1)}, u32[]{:S(2)}, u32[]{:S(2)}) collective-permute-start(bf16[2,4,2,8,896]{4,3,2,1,0:T(8,128)(2,1)S(1)} %get-tuple-element.121), channel_id=1, source_target_pairs={{0,8},{1,9},{2,10},{3,11},{4,12},{5,13},{6,14},{7,15},{8,0},{9,1},... | collective-permute-start | bytes 688136 | tf_op jit(solution)/shard_map/ppermute | solution.py:652
  23.5 10.5 %copy-start.11 = (f32[1,768]{1,0:T(1,128)}, f32[1,768]{1,0:T(1,128)S(1)}, u32[]{:S(2)}) copy-start(f32[1,768]{1,0:T(1,128)S(1)} %reshape.150.gain) | copy-start | bytes 9220
  34.0 1.0 copy-start.3
  35.0 0.9 copy-start.5
  35.9 0.7 copy-start.7
  36.6 0.7 copy-start.9
  173.0 25.2 %copy-start.13 = (s32[2]{0:T(128)S(1)}, s32[2]{0:T(128)}, u32[]{:S(2)}) copy-start(s32[2]{0:T(128)} %pad_add_fusion.ids) | copy-start | bytes 28
  173.0 25.2 %copy-start.14 = (bf16[8,208,768]{2,1,0:T(8,128)(2,1)S(1)}, bf16[8,208,768]{2,1,0:T(8,128)(2,1)}, u32[]{:S(2)}) copy-start(bf16[8,208,768]{2,1,0:T(8,128)(2,1)} %get-tuple-element.73) | copy-start | bytes 7667716
  189.4 6.0 %collective-permute-start.8 = (bf16[16,768]{1,0:T(8,128)(2,1)}, bf16[16,768]{1,0:T(8,128)(2,1)S(1)}, u32[]{:S(2)}, u32[]{:S(2)}) collective-permute-start(bf16[16,768]{1,0:T(8,128)(2,1)} %get-tuple-element.62), channel_id=1, source_target_pairs={{0,6},{1,7},{2,4},{3,5},{4,2},{5,3},{6,0},{7,1},{8,14},{9,15},{10,... | collective-permute-start | bytes 73736 | tf_op jit(solution)/shard_map/ppermute | solution.py:652
  189.6 5.9 %collective-permute-start.7 = (bf16[16,768]{1,0:T(8,128)(2,1)}, bf16[16,768]{1,0:T(8,128)(2,1)S(1)}, u32[]{:S(2)}, u32[]{:S(2)}) collective-permute-start(bf16[16,768]{1,0:T(8,128)(2,1)} %get-tuple-element.62), channel_id=1, source_target_pairs={{0,4},{1,5},{2,6},{3,7},{4,0},{5,1},{6,2},{7,3},{8,12},{9,13},{10,... | collective-permute-start | bytes 73736 | tf_op jit(solution)/shard_map/ppermute | solution.py:652
  189.6 6.3 %collective-permute-start.6 = (bf16[16,768]{1,0:T(8,128)(2,1)}, bf16[16,768]{1,0:T(8,128)(2,1)S(1)}, u32[]{:S(2)}, u32[]{:S(2)}) collective-permute-start(bf16[16,768]{1,0:T(8,128)(2,1)} %get-tuple-element.62), channel_id=1, source_target_pairs={{0,2},{1,3},{2,0},{3,1},{4,6},{5,7},{6,4},{7,5},{8,10},{9,11},{10,... | collective-permute-start | bytes 73736 | tf_op jit(solution)/shard_map/ppermute | solution.py:652
  193.8 24.0 %collective-permute-start.29 = (bf16[8,1,96,384]{3,2,1,0:T(8,128)(2,1)}, bf16[8,1,96,384]{3,2,1,0:T(8,128)(2,1)}, u32[]{:S(2)}, u32[]{:S(2)}) collective-permute-start(bf16[8,1,96,384]{3,2,1,0:T(8,128)(2,1)} %get-tuple-element.81), channel_id=1, source_target_pairs={{0,8},{1,9},{2,10},{3,11},{4,12},{5,13},{6,14},{7,15},{8,0},{9,1},... | collective-permute-start | bytes 1769480 | tf_op jit(solution)/shard_map/ppermute | solution.py:652
  193.8 44.7 %collective-permute-start.19 = (bf16[8,4,96,384]{3,2,1,0:T(8,128)(2,1)}, bf16[8,4,96,384]{3,2,1,0:T(8,128)(2,1)}, u32[]{:S(2)}, u32[]{:S(2)}) collective-permute-start(bf16[8,4,96,384]{3,2,1,0:T(8,128)(2,1)} %get-tuple-element.77), channel_id=1, source_target_pairs={{0,8},{1,9},{2,10},{3,11},{4,12},{5,13},{6,14},{7,15},{8,0},{9,1},... | collective-permute-start | bytes 7077896 | tf_op jit(solution)/shard_map/ppermute | solution.py:652
  196.6 12.9 %collective-permute-start.9 = (bf16[4,16,768]{2,1,0:T(8,128)(2,1)S(1)}, bf16[4,16,768]{2,1,0:T(8,128)(2,1)S(1)}, u32[]{:S(2)}, u32[]{:S(2)}) collective-permute-start(bf16[4,16,768]{2,1,0:T(8,128)(2,1)S(1)} %get-tuple-element.129), channel_id=1, source_target_pairs={{0,16},{1,17},{2,18},{3,19},{4,20},{5,21},{6,22},{7,23},{8,24},{9,... | collective-permute-start | bytes 294920 | tf_op jit(solution)/shard_map/ppermute | solution.py:652
  198.2 19.6 %copy-start.18 = (bf16[8,1,96,384]{3,2,1,0:T(8,128)(2,1)S(1)}, bf16[8,1,96,384]{3,2,1,0:T(8,128)(2,1)}, u32[]{:S(2)}) copy-start(bf16[8,1,96,384]{3,2,1,0:T(8,128)(2,1)} %get-tuple-element.80) | copy-start | bytes 1769476
  208.4 1.2 copy-start.1
  209.6 26.7 %collective-permute-start.12 = (bf16[8,3,96,384]{3,2,1,0:T(8,128)(2,1)}, bf16[8,3,96,384]{3,2,1,0:T(8,128)(2,1)}, u32[]{:S(2)}, u32[]{:S(2)}) collective-permute-start(bf16[8,3,96,384]{3,2,1,0:T(8,128)(2,1)} %get-tuple-element.75), channel_id=1, source_target_pairs={{0,8},{1,9},{2,10},{3,11},{4,12},{5,13},{6,14},{7,15},{8,0},{9,1},... | collective-permute-start | bytes 5308424 | tf_op jit(solution)/shard_map/ppermute | solution.py:652
  209.6 7.4 %collective-permute-start.10 = (bf16[4,2,16,768]{3,2,0,1:T(8,128)(2,1)S(1)}, bf16[4,2,16,768]{3,2,0,1:T(8,128)(2,1)S(1)}, u32[]{:S(2)}, u32[]{:S(2)}) collective-permute-start(bf16[4,2,16,768]{3,2,0,1:T(8,128)(2,1)S(1)} %get-tuple-element.123), channel_id=1, source_target_pairs={{0,1},{1,0},{2,3},{3,2},{4,5},{5,4},{6,7},{7,6},{8,9},{9,8},{10,11... | collective-permute-start | bytes 589832 | tf_op jit(solution)/shard_map/ppermute | solution.py:652
  211.2 33.7 %collective-permute-start.24 = (bf16[8,1,384,384]{3,2,0,1:T(8,128)(2,1)}, bf16[8,1,384,384]{3,2,0,1:T(8,128)(2,1)}, u32[]{:S(2)}, u32[]{:S(2)}) collective-permute-start(bf16[8,1,384,384]{3,2,0,1:T(8,128)(2,1)} %bitcast.48), channel_id=1, source_target_pairs={{0,8},{1,9},{2,10},{3,11},{4,12},{5,13},{6,14},{7,15},{8,0},{9,1},... | collective-permute-start | bytes 7077896 | tf_op jit(solution)/shard_map/ppermute | solution.py:652
  217.8 3.5 collective-permute-start.11
  217.8 5.5 %copy-start.4 = (bf16[256,2304]{1,0:T(8,128)(2,1)S(1)}, bf16[256,2304]{1,0:T(8,128)(2,1)}, u32[]{:S(2)}) copy-start(bf16[256,2304]{1,0:T(8,128)(2,1)} %copy-done.3) | copy-start | bytes 3538948
  217.8 5.5 %copy-start.6 = (f32[256,768]{1,0:T(8,128)S(1)}, f32[256,768]{1,0:T(8,128)}, u32[]{:S(2)}) copy-start(f32[256,768]{1,0:T(8,128)} %copy-done.5) | copy-start | bytes 2359300
  217.8 5.5 %copy-start.8 = (bf16[256,768]{1,0:T(8,128)(2,1)S(1)}, bf16[256,768]{1,0:T(8,128)(2,1)}, u32[]{:S(2)}) copy-start(bf16[256,768]{1,0:T(8,128)(2,1)} %copy-done.7) | copy-start | bytes 1179652
  217.8 5.5 %copy-start.10 = (f32[256,128]{1,0:T(8,128)S(1)}, f32[256,128]{1,0:T(8,128)}, u32[]{:S(2)}) copy-start(f32[256,128]{1,0:T(8,128)} %copy-done.9) | copy-start | bytes 393220
  217.8 5.5 %copy-start.12 = (f32[1,768]{1,0:T(1,128)S(1)}, f32[1,768]{1,0:T(1,128)}, u32[]{:S(2)}) copy-start(f32[1,768]{1,0:T(1,128)} %copy-done.11) | copy-start | bytes 9220
  219.8 21.9 %collective-permute-start.30 = (bf16[4,1,96,384]{3,2,1,0:T(8,128)(2,1)}, bf16[4,1,96,384]{3,2,1,0:T(8,128)(2,1)}, u32[]{:S(2)}, u32[]{:S(2)}) collective-permute-start(bf16[4,1,96,384]{3,2,1,0:T(8,128)(2,1)} %add_convert_fusion.4), channel_id=1, source_target_pairs={{0,1},{1,0},{2,3},{3,2},{4,5},{5,4},{6,7},{7,6},{8,9},{9,8},{10,11... | collective-permute-start | bytes 884744 | tf_op jit(solution)/shard_map/ppermute | solution.py:652
  222.4 0.9 copy-start.17
  233.6 4.9 %copy-start.16 = (bf16[8,4,96,384]{3,2,1,0:T(8,128)(2,1)S(1)}, bf16[8,4,96,384]{3,2,1,0:T(8,128)(2,1)}, u32[]{:S(2)}) copy-start(bf16[8,4,96,384]{3,2,1,0:T(8,128)(2,1)} %get-tuple-element.76) | copy-start | bytes 7077892
  237.9 3.8 %copy-start.19 = (bf16[8,1,96,384]{3,2,1,0:T(8,128)(2,1)S(1)}, bf16[8,1,96,384]{3,2,1,0:T(8,128)(2,1)}, u32[]{:S(2)}) copy-start(bf16[8,1,96,384]{3,2,1,0:T(8,128)(2,1)} %get-tuple-element.80) | copy-start | bytes 1769476
  237.9 7.0 %copy-start.15 = (bf16[2,4,384,384]{3,2,1,0:T(8,128)(2,1)S(1)}, bf16[2,4,384,384]{3,2,1,0:T(8,128)(2,1)}, u32[]{:S(2)}) copy-start(bf16[2,4,384,384]{3,2,1,0:T(8,128)(2,1)} %get-tuple-element.78) | copy-start | bytes 7077892
  237.9 22.6 %collective-permute-start.13 = (bf16[4,3,96,384]{3,2,1,0:T(8,128)(2,1)S(1)}, bf16[4,3,96,384]{3,2,1,0:T(8,128)(2,1)S(1)}, u32[]{:S(2)}, u32[]{:S(2)}) collective-permute-start(bf16[4,3,96,384]{3,2,1,0:T(8,128)(2,1)S(1)} %add_convert_fusion.1), channel_id=1, source_target_pairs={{0,1},{1,0},{2,3},{3,2},{4,5},{5,4},{6,7},{7,6},{8,9},{9,8},{10,11... | collective-permute-start | bytes 2654216 | tf_op jit(solution)/shard_map/ppermute | solution.py:652
  240.3 20.1 %copy-start.2 = (bf16[8,3,96,384]{3,2,1,0:T(8,128)(2,1)S(1)}, bf16[8,3,96,384]{3,2,1,0:T(8,128)(2,1)}, u32[]{:S(2)}) copy-start(bf16[8,3,96,384]{3,2,1,0:T(8,128)(2,1)} %copy-done.1) | copy-start | bytes 5308420
  240.4 45.4 %collective-permute-start.20 = (bf16[4,4,96,384]{3,2,1,0:T(8,128)(2,1)S(1)}, bf16[4,4,96,384]{3,2,1,0:T(8,128)(2,1)S(1)}, u32[]{:S(2)}, u32[]{:S(2)}) collective-permute-start(bf16[4,4,96,384]{3,2,1,0:T(8,128)(2,1)S(1)} %add_convert_fusion), channel_id=1, source_target_pairs={{0,1},{1,0},{2,3},{3,2},{4,5},{5,4},{6,7},{7,6},{8,9},{9,8},{10,11... | collective-permute-start | bytes 3538952 | tf_op jit(solution)/shard_map/ppermute | solution.py:652
  242.8 5.5 %collective-permute-start.31 = (bf16[1,1,96,384]{3,2,1,0:T(8,128)(2,1)S(1)}, bf16[1,1,96,384]{3,2,1,0:T(8,128)(2,1)S(1)}, u32[]{:S(2)}, u32[]{:S(2)}) collective-permute-start(bf16[1,1,96,384]{3,2,1,0:T(8,128)(2,1)S(1)} %get-tuple-element.109), channel_id=1, source_target_pairs={{0,2},{1,3},{2,0},{3,1},{4,6},{5,7},{6,4},{7,5},{8,10},{9,11},{10,... | collective-permute-start | bytes 221192 | tf_op jit(solution)/shard_map/ppermute | solution.py:652
  246.5 63.8 %collective-permute-start.25 = (bf16[4,1,384,384]{3,2,0,1:T(8,128)(2,1)S(1)}, bf16[4,1,384,384]{3,2,0,1:T(8,128)(2,1)S(1)}, u32[]{:S(2)}, u32[]{:S(2)}) collective-permute-start(bf16[4,1,384,384]{3,2,0,1:T(8,128)(2,1)S(1)} %fusion), channel_id=1, source_target_pairs={{0,1},{1,0},{2,3},{3,2},{4,5},{5,4},{6,7},{7,6},{8,9},{9,8},{10,11... | collective-permute-start | bytes 3538952 | tf_op jit(solution)/shard_map/ppermute | solution.py:652
  247.9 6.2 %collective-permute-start.33 = (bf16[1,1,96,384]{3,2,1,0:T(8,128)(2,1)S(1)}, bf16[1,1,96,384]{3,2,1,0:T(8,128)(2,1)S(1)}, u32[]{:S(2)}, u32[]{:S(2)}) collective-permute-start(bf16[1,1,96,384]{3,2,1,0:T(8,128)(2,1)S(1)} %get-tuple-element.110), channel_id=1, source_target_pairs={{0,6},{1,7},{2,4},{3,5},{4,2},{5,3},{6,0},{7,1},{8,14},{9,15},{10,... | collective-permute-start | bytes 221192 | tf_op jit(solution)/shard_map/ppermute | solution.py:652
  248.3 8.1 %collective-permute-start.32 = (bf16[1,1,96,384]{3,2,1,0:T(8,128)(2,1)S(1)}, bf16[1,1,96,384]{3,2,1,0:T(8,128)(2,1)S(1)}, u32[]{:S(2)}, u32[]{:S(2)}) collective-permute-start(bf16[1,1,96,384]{3,2,1,0:T(8,128)(2,1)S(1)} %get-tuple-element.111), channel_id=1, source_target_pairs={{0,4},{1,5},{2,6},{3,7},{4,0},{5,1},{6,2},{7,3},{8,12},{9,13},{10,... | collective-permute-start | bytes 221192 | tf_op jit(solution)/shard_map/ppermute | solution.py:652
  261.9 27.4 %collective-permute-start.14 = (bf16[1,3,96,384]{3,2,1,0:T(8,128)(2,1)S(1)}, bf16[1,3,96,384]{3,2,1,0:T(8,128)(2,1)S(1)}, u32[]{:S(2)}, u32[]{:S(2)}) collective-permute-start(bf16[1,3,96,384]{3,2,1,0:T(8,128)(2,1)S(1)} %get-tuple-element.106), channel_id=1, source_target_pairs={{0,2},{1,3},{2,0},{3,1},{4,6},{5,7},{6,4},{7,5},{8,10},{9,11},{10,... | collective-permute-start | bytes 663560 | tf_op jit(solution)/shard_map/ppermute | solution.py:652
  263.9 25.3 %collective-permute-start.16 = (bf16[1,3,96,384]{3,2,1,0:T(8,128)(2,1)S(1)}, bf16[1,3,96,384]{3,2,1,0:T(8,128)(2,1)S(1)}, u32[]{:S(2)}, u32[]{:S(2)}) collective-permute-start(bf16[1,3,96,384]{3,2,1,0:T(8,128)(2,1)S(1)} %get-tuple-element.107), channel_id=1, source_target_pairs={{0,6},{1,7},{2,4},{3,5},{4,2},{5,3},{6,0},{7,1},{8,14},{9,15},{10,... | collective-permute-start | bytes 663560 | tf_op jit(solution)/shard_map/ppermute | solution.py:652
  264.4 24.9 %collective-permute-start.15 = (bf16[1,3,96,384]{3,2,1,0:T(8,128)(2,1)S(1)}, bf16[1,3,96,384]{3,2,1,0:T(8,128)(2,1)S(1)}, u32[]{:S(2)}, u32[]{:S(2)}) collective-permute-start(bf16[1,3,96,384]{3,2,1,0:T(8,128)(2,1)S(1)} %get-tuple-element.108), channel_id=1, source_target_pairs={{0,4},{1,5},{2,6},{3,7},{4,0},{5,1},{6,2},{7,3},{8,12},{9,13},{10,... | collective-permute-start | bytes 663560 | tf_op jit(solution)/shard_map/ppermute | solution.py:652
  287.2 27.1 %collective-permute-start.21 = (bf16[1,4,96,384]{3,2,1,0:T(8,128)(2,1)S(1)}, bf16[1,4,96,384]{3,2,1,0:T(8,128)(2,1)S(1)}, u32[]{:S(2)}, u32[]{:S(2)}) collective-permute-start(bf16[1,4,96,384]{3,2,1,0:T(8,128)(2,1)S(1)} %get-tuple-element.103), channel_id=1, source_target_pairs={{0,2},{1,3},{2,0},{3,1},{4,6},{5,7},{6,4},{7,5},{8,10},{9,11},{10,... | collective-permute-start | bytes 884744 | tf_op jit(solution)/shard_map/ppermute | solution.py:652
  290.4 23.5 %collective-permute-start.17 = (bf16[3,96,384]{2,1,0:T(8,128)(2,1)S(1)}, bf16[3,96,384]{2,1,0:T(8,128)(2,1)S(1)}, u32[]{:S(2)}, u32[]{:S(2)}) collective-permute-start(bf16[3,96,384]{2,1,0:T(8,128)(2,1)S(1)} %fusion.3), channel_id=1, source_target_pairs={{0,16},{1,17},{2,18},{3,19},{4,20},{5,21},{6,22},{7,23},{8,24},{9,... | collective-permute-start | bytes 663560 | tf_op jit(solution)/shard_map/ppermute | solution.py:652
  291.0 24.5 %collective-permute-start.23 = (bf16[1,4,96,384]{3,2,1,0:T(8,128)(2,1)S(1)}, bf16[1,4,96,384]{3,2,1,0:T(8,128)(2,1)S(1)}, u32[]{:S(2)}, u32[]{:S(2)}) collective-permute-start(bf16[1,4,96,384]{3,2,1,0:T(8,128)(2,1)S(1)} %get-tuple-element.104), channel_id=1, source_target_pairs={{0,6},{1,7},{2,4},{3,5},{4,2},{5,3},{6,0},{7,1},{8,14},{9,15},{10,... | collective-permute-start | bytes 884744 | tf_op jit(solution)/shard_map/ppermute | solution.py:652
  291.3 26.6 %collective-permute-start.22 = (bf16[1,4,96,384]{3,2,1,0:T(8,128)(2,1)S(1)}, bf16[1,4,96,384]{3,2,1,0:T(8,128)(2,1)S(1)}, u32[]{:S(2)}, u32[]{:S(2)}) collective-permute-start(bf16[1,4,96,384]{3,2,1,0:T(8,128)(2,1)S(1)} %get-tuple-element.105), channel_id=1, source_target_pairs={{0,4},{1,5},{2,6},{3,7},{4,0},{5,1},{6,2},{7,3},{8,12},{9,13},{10,... | collective-permute-start | bytes 884744 | tf_op jit(solution)/shard_map/ppermute | solution.py:652
  311.8 17.5 %collective-permute-start.26 = (bf16[1,1,384,384]{3,2,0,1:T(8,128)(2,1)S(1)}, bf16[1,1,384,384]{3,2,0,1:T(8,128)(2,1)S(1)}, u32[]{:S(2)}, u32[]{:S(2)}) collective-permute-start(bf16[1,1,384,384]{3,2,0,1:T(8,128)(2,1)S(1)} %get-tuple-element.100), channel_id=1, source_target_pairs={{0,2},{1,3},{2,0},{3,1},{4,6},{5,7},{6,4},{7,5},{8,10},{9,11},{10,... | collective-permute-start | bytes 884744 | tf_op jit(solution)/shard_map/ppermute | solution.py:652
  313.9 15.5 %collective-permute-start.28 = (bf16[1,1,384,384]{3,2,0,1:T(8,128)(2,1)S(1)}, bf16[1,1,384,384]{3,2,0,1:T(8,128)(2,1)S(1)}, u32[]{:S(2)}, u32[]{:S(2)}) collective-permute-start(bf16[1,1,384,384]{3,2,0,1:T(8,128)(2,1)S(1)} %get-tuple-element.101), channel_id=1, source_target_pairs={{0,6},{1,7},{2,4},{3,5},{4,2},{5,3},{6,0},{7,1},{8,14},{9,15},{10,... | collective-permute-start | bytes 884744 | tf_op jit(solution)/shard_map/ppermute | solution.py:652
  314.3 27.7 %collective-permute-start.27 = (bf16[1,1,384,384]{3,2,0,1:T(8,128)(2,1)S(1)}, bf16[1,1,384,384]{3,2,0,1:T(8,128)(2,1)S(1)}, u32[]{:S(2)}, u32[]{:S(2)}) collective-permute-start(bf16[1,1,384,384]{3,2,0,1:T(8,128)(2,1)S(1)} %get-tuple-element.102), channel_id=1, source_target_pairs={{0,4},{1,5},{2,6},{3,7},{4,0},{5,1},{6,2},{7,3},{8,12},{9,13},{10,... | collective-permute-start | bytes 884744 | tf_op jit(solution)/shard_map/ppermute | solution.py:652
  315.5 29.8 %collective-permute-start.18 = (bf16[3,96,384]{2,1,0:T(8,128)(2,1)S(1)}, bf16[3,96,384]{2,1,0:T(8,128)(2,1)S(1)}, u32[]{:S(2)}, u32[]{:S(2)}) collective-permute-start(bf16[3,96,384]{2,1,0:T(8,128)(2,1)S(1)} %add_convert_fusion.13), channel_id=1, source_target_pairs={{0,8},{1,9},{2,10},{3,11},{4,12},{5,13},{6,14},{7,15},{8,0},{9,1},... | collective-permute-start | bytes 663560 | tf_op jit(solution)/shard_map/ppermute | solution.py:652
  343.2 5.3 %collective-permute-start.36 = (bf16[1,96,384]{2,1,0:T(8,128)(2,1)S(1)}, bf16[1,96,384]{2,1,0:T(8,128)(2,1)S(1)}, u32[]{:S(2)}, u32[]{:S(2)}) collective-permute-start(bf16[1,96,384]{2,1,0:T(8,128)(2,1)S(1)} %fusion.4), channel_id=1, source_target_pairs={{0,16},{1,17},{2,18},{3,19},{4,20},{5,21},{6,22},{7,23},{8,24},{9,... | collective-permute-start | bytes 221192 | tf_op jit(solution)/shard_map/ppermute | solution.py:652
  344.8 10.0 %collective-permute-start.34 = (bf16[4,96,384]{2,1,0:T(8,128)(2,1)S(1)}, bf16[4,96,384]{2,1,0:T(8,128)(2,1)S(1)}, u32[]{:S(2)}, u32[]{:S(2)}) collective-permute-start(bf16[4,96,384]{2,1,0:T(8,128)(2,1)S(1)} %fusion.1), channel_id=1, source_target_pairs={{0,16},{1,17},{2,18},{3,19},{4,20},{5,21},{6,22},{7,23},{8,24},{9,... | collective-permute-start | bytes 884744 | tf_op jit(solution)/shard_map/ppermute | solution.py:652
  345.3 13.6 %collective-permute-start.35 = (bf16[1,384,384]{2,1,0:T(8,128)(2,1)S(1)}, bf16[1,384,384]{2,1,0:T(8,128)(2,1)S(1)}, u32[]{:S(2)}, u32[]{:S(2)}) collective-permute-start(bf16[1,384,384]{2,1,0:T(8,128)(2,1)S(1)} %fusion.2), channel_id=1, source_target_pairs={{0,16},{1,17},{2,18},{3,19},{4,20},{5,21},{6,22},{7,23},{8,24},{9,... | collective-permute-start | bytes 884744 | tf_op jit(solution)/shard_map/ppermute | solution.py:652
  359.0 3.2 collective-permute-start.37
  361.7 4.0 %collective-permute-start.38 = (bf16[4,96,384]{2,1,0:T(8,128)(2,1)S(1)}, bf16[4,96,384]{2,1,0:T(8,128)(2,1)S(1)}, u32[]{:S(2)}, u32[]{:S(2)}) collective-permute-start(bf16[4,96,384]{2,1,0:T(8,128)(2,1)S(1)} %add_convert_fusion.3), channel_id=1, source_target_pairs={{0,8},{1,9},{2,10},{3,11},{4,12},{5,13},{6,14},{7,15},{8,0},{9,1},... | collective-permute-start | bytes 884744 | tf_op jit(solution)/shard_map/ppermute | solution.py:652
  362.2 1.6 collective-permute-start.39
